TPU v7x, 512 devices: a whole 4x4x16 slice. The times are simulated.
512 devices in a mesh: env: 32 (over z, core), sp: 16 (over x, y).
Axes of the slice: x: 4, y: 4, z: 16, core: 2. Of those that a mesh axis runs over, the one named last changes fastest.
Arguments:
- env_desc: bfloat16 [32768, 1000], P('env'), may hold values from -6 to 6
- env_counts: int32 [32, 448], P('env'), may hold values from 1 to 6, 1024 in all within a row
- reg_desc: bfloat16 [2048, 1000], P('env'), may hold values from -6 to 6
- sparse_desc: bfloat16 [80, 256, 1000], P('sp', 'env'), may hold values from -6 to 6
- panel_block: int32 [], replicated, may hold values from 0 to 79
Outputs:
- updated: float32 [16384, 20480], P('env', 'sp')
- coupling: float32 [256, 20480], P(None, 'sp')
Inputs may be any that keep to these rules, and one draw needn't show every extreme that they name: Each row of env_counts sums to 1024, and its largest entry is 6.
All inputs are finite; a program needn't handle non-finite values.
Results may differ from a plain program's by a relative error of at most 0.0003.
Values may be sent and summed in bfloat16 or wider, within the bound.
No kernel may reach another device: no remote copies, remote signals or barrier semaphores. Data moves between devices by JAX's collectives and lax.ppermute only.
A program may use at most 64 MiB of HBM per device.

v0:
```python
import math

import jax
import jax.numpy as jnp
from jax import lax
from jax.sharding import PartitionSpec as P

DESC = 1000
PANEL = 256


cube_scale = 15.0 ** (-0.5)


def from_root(block, axis, owner):
    block = jnp.where(lax.axis_index(axis) == owner, block, jnp.zeros_like(block))
    return lax.psum(block, axis)


def kernel(left_desc, right_desc):
    scaled = lax.dot_general(
        left_desc, right_desc, (((1,), (1,)), ((), ())), preferred_element_type=jnp.float32
    ) * DESC ** (-0.5)
    return scaled * scaled * scaled * cube_scale


def energy_rows(counts, kernel_rows):
    conf_count = counts.shape[0]
    env_count = kernel_rows.shape[0]
    group = math.gcd(conf_count, 64)
    most_envs = 3 * env_count // conf_count
    window = min(group * most_envs, env_count)
    finish = jnp.cumsum(counts)
    starts = finish - counts
    grouped = (
        counts.reshape(conf_count // group, group),
        starts.reshape(conf_count // group, group),
        finish.reshape(conf_count // group, group),
    )

    def one_group(pieces):
        group_counts, group_starts, group_finish = pieces
        begin = jnp.minimum(group_starts[0], env_count - window)
        rows_window = lax.dynamic_slice_in_dim(kernel_rows, begin, window, 0)
        position = begin + jnp.arange(window, dtype=jnp.int32)[None, :]
        member = ((position >= group_starts[:, None]) & (position < group_finish[:, None])).astype(
            jnp.float32
        )
        weights = member / group_counts.astype(jnp.float32)[:, None]
        return jnp.dot(weights, rows_window, precision=lax.Precision.HIGHEST)

    blocks = lax.map(one_group, grouped)
    return blocks.reshape(conf_count, kernel_rows.shape[1])


def cross_gram(left_cols, right_cols):
    return lax.dot_general(
        left_cols, right_cols, (((0,), (0,)), ((), ())), precision=lax.Precision.HIGHEST
    )


def shards(env_desc, env_counts, reg_desc, sparse_desc, panel_block):
    gathered = lax.all_gather(sparse_desc, "env", axis=1, tiled=True)
    points = gathered.reshape(gathered.shape[0] * gathered.shape[1], gathered.shape[2])
    counts = env_counts[0]
    col_count = points.shape[0]
    offset = panel_block * PANEL
    owner_index = offset // col_count
    local_start = offset - owner_index * col_count
    column_shard = lax.axis_index("sp")
    kernel_rows = kernel(env_desc, points)
    design = jnp.concatenate([energy_rows(counts, kernel_rows), kernel(reg_desc, points)], 0)
    panel_cols = lax.dynamic_slice_in_dim(design, local_start, PANEL, 1)
    panel_cols = from_root(panel_cols, "sp", owner_index)
    gram_matrix = lax.psum(cross_gram(panel_cols, panel_cols), "env")
    lower_factor = jnp.linalg.cholesky(gram_matrix)
    orthogonal = jax.scipy.linalg.solve_triangular(lower_factor, panel_cols.T, lower=True).T
    coupling = lax.psum(cross_gram(orthogonal, design), "env")
    column = column_shard * col_count + jnp.arange(col_count, dtype=jnp.int32)
    coupling = jnp.where(column[None, :] >= offset, coupling, jnp.zeros_like(coupling))
    updated = design - jnp.dot(orthogonal, coupling, precision=lax.Precision.HIGHEST)
    placed = lax.dynamic_update_slice_in_dim(updated, orthogonal, local_start, 1)
    updated = jnp.where(column_shard == owner_index, placed, updated)
    return (updated, coupling)


def solution(mesh):
    in_specs = (P("env", None), P("env", None), P("env", None), P("sp", "env", None), P())
    out_specs = (P("env", "sp"), P(None, "sp"))
    return jax.shard_map(shards, mesh=mesh, in_specs=in_specs, out_specs=out_specs, check_vma=False)
```

profile of v0, /device:TPU:1, one launch (start us, length us, event | category | flops | bytes accessed | tf_op | source)
XLA Modules:
  0.0 762.3 jit_solution(6687802489376797020)
XLA Ops:
  10.6 1.3 reduce.17
  12.1 76.3 %all-gather.2.cloned.1.call-done = bf16[5,256,1000]{2,1,0:T(8,128)(2,1)} async-done(((bf16[5,8,1000]{2,1,0:T(8,128)(2,1)}), bf16[5,256,1000]{2,1,0:T(8,128)(2,1)}) %all-gather.2.cloned.1.call-update) | async-done | bytes 2560016 | tf_op jit(solution)/shard_map/all_gather | solution.py:63
  88.4 2.7 fusion.20
  91.4 6.7 fusion.15
  98.1 26.8 %while.11 = (s32[]{:T(128)}, f32[7,64,1280]{2,1,0:T(8,128)}, s32[7,64]{1,0:T(8,128)S(1)}, s32[7,64]{1,0:T(8,128)S(1)}, s32[7,64]{1,0:T(8,128)S(1)}, /*index=5*/f...) while((s32[]{:T(128)}, f32[7,64,1280]{2,1,0:T(8,128)}, s32[7,64]{1,0:T(8,128)S(1)}, ...), condition=%wide.region_3.4_spmd, body=%wide.region_2.3_spmd.sunk | while | flops 377610688 | bytes 2299827 | solution.py:52
  98.2 3.7 fusion.56
  102.0 3.8 fusion.56
  105.9 3.7 fusion.56
  109.7 3.7 fusion.56
  113.6 3.7 fusion.56
  117.4 3.7 fusion.56
  121.2 3.7 fusion.56
  124.9 3.2 copy.13
  128.1 1.9 fusion.18
  130.1 111.3 %all-reduce.6.cloned.1.call-done = f32[512,256]{0,1:T(8,128)} async-done(((f32[512,256]{0,1:T(8,128)}), f32[512,256]{0,1:T(8,128)}) %all-reduce.6.cloned.1.call-update) | async-done | bytes 524304 | tf_op jit(solution)/shard_map/psum | solution.py:17
  241.4 2.6 fusion.33
  244.8 206.6 %all-reduce.8.cloned.1.call-done = f32[256,256]{0,1:T(8,128)} async-done(((f32[256,256]{0,1:T(8,128)}), f32[256,256]{0,1:T(8,128)}) %all-reduce.8.cloned.1.call-update) | async-done | bytes 262160 | tf_op jit(solution)/shard_map/psum | solution.py:75
  454.2 11.7 %cholesky.50 = f32[128,128]{1,0:T(8,128)S(1)} custom-call(f32[128,128]{1,0:T(8,128)S(1)} %cholesky.118), custom_call_target="Cholesky" | custom-call | tf_op jit(solution)/shard_map/jit(cholesky)/cholesky | solution.py:76
  467.1 10.6 %custom-call.15 = f32[1,128,128]{1,2,0:T(8,128)S(1)} custom-call(f32[1,128,128]{2,1,0:T(8,128)} %get-tuple-element.74), custom_call_target="InvertDiagBlocksLowerTriangular" | custom-call | tf_op jit(solution)/shard_map/jit(cholesky)/cholesky | solution.py:76
  478.8 1.7 convolution_subtract_fusion.2
  480.5 12.5 %cholesky.105 = f32[128,128]{1,0:T(8,128)S(1)} custom-call(f32[128,128]{1,0:T(8,128)} %convolution_subtract_fusion.2), custom_call_target="Cholesky" | custom-call | tf_op jit(solution)/shard_map/jit(cholesky)/cholesky | solution.py:76
  493.1 1.3 compare_reduce_fusion
  497.4 5.3 while.12
  498.0 2.0 bitcast_dynamic-update-slice_fusion.2
  500.7 2.0 bitcast_dynamic-update-slice_fusion.2
  502.7 21.1 %custom-call.16 = f32[2,128,128]{1,2,0:T(8,128)} custom-call(f32[2,128,128]{2,1,0:T(8,128)} %get-tuple-element.42), custom_call_target="InvertDiagBlocksLowerTriangular" | custom-call | tf_op jit(solution)/shard_map/jit(_solve_triangular)/triangular_solve | solution.py:77
  527.6 5.1 fusion.16
  532.8 211.5 %all-reduce.10.cloned.1.call-done = f32[256,1280]{1,0:T(8,128)} async-done(((f32[256,1280]{1,0:T(8,128)}), f32[256,1280]{1,0:T(8,128)}) %all-reduce.10.cloned.1.call-update) | async-done | bytes 1310736 | tf_op jit(solution)/shard_map/psum | solution.py:78
  744.3 1.6 broadcast_select_fusion
  746.5 4.1 convolution_subtract_fusion
  750.6 1.9 fusion.19
  752.6 3.2 copy.18
  (83 shorter events, 16.4 us)
Async XLA Ops:
  7.2 84.3 %copy-start = (bf16[1024,1000]{0,1:T(8,128)(2,1)S(1)}, bf16[1024,1000]{0,1:T(8,128)(2,1)}, u32[]{:S(2)}) copy-start(bf16[1024,1000]{0,1:T(8,128)(2,1)} %param.7) | copy-start | bytes 6144004
  7.2 81.3 %all-gather.2.cloned.1.call-start = ((), (), s32[]{:S(2)}) async-start(), calls=%async_computation | async-start | bytes 2703360 | tf_op jit(solution)/shard_map/all_gather | solution.py:63
  7.9 233.5 %all-reduce.6.cloned.1.call-start = ((), (), s32[]{:S(2)}) async-start(), calls=%async_computation.1 | async-start | bytes 1048576 | tf_op jit(solution)/shard_map/psum | solution.py:17
  130.0 321.4 %all-reduce.8.cloned.1.call-start = ((), (), s32[]{:S(2)}) async-start(), calls=%async_computation.2 | async-start | bytes 524288 | tf_op jit(solution)/shard_map/psum | solution.py:75
  241.4 282.5 %copy-start.3 = (f32[512,256]{0,1:T(8,128)S(1)}, f32[512,256]{0,1:T(8,128)}, u32[]{:S(2)}) copy-start(f32[512,256]{0,1:T(8,128)} %all-reduce.6.cloned.1.call-done) | copy-start | bytes 1572868
  244.0 500.3 %all-reduce.10.cloned.1.call-start = ((), (), s32[]{:S(2)}) async-start(), calls=%async_computation.3 | async-start | bytes 2621440 | tf_op jit(solution)/shard_map/psum | solution.py:78
  453.5 0.7 copy-start.6
  493.1 2.6 copy-start.5
  502.7 21.1 %copy-start.4 = (f32[256,256]{1,0:T(8,128)}, f32[256,256]{1,0:T(8,128)S(1)}, u32[]{:S(2)}) copy-start(f32[256,256]{1,0:T(8,128)S(1)} %get-tuple-element.206) | copy-start | bytes 786436
  744.3 2.1 copy-start.1
  746.5 4.1 copy-start.2
Sparse Core Ops, SparseCore 0:
  10.2 78.2 all-gather.1
  130.2 111.2 all-reduce.5
  244.4 206.9 all-reduce.7
  532.9 211.3 all-reduce.9
where the time goes:
time: 764 us; the launch traced here: 762 us
  waiting for transfers between devices  607 us (79%)
  other arithmetic  68.4 us (9%)
  matrix products  53.8 us (7%)
  local copies, waits for them, and re-layouts  16.8 us (2%)
  between operations  15.9 us (2%)
    psum x1, waiting for transfers between devices, shards(): coupling = lax.psum(cross_gram(orthogonal, design), 'env')  212 us
    psum x1, waiting for transfers between devices, shards(): gram_matrix = lax.psum(cross_gram(panel_cols, panel_cols), 'env')  207 us
    psum x1, waiting for transfers between devices, from_root(): return lax.psum(block, axis)  111 us
    all_gather x1, waiting for transfers between devices, shards(): gathered = lax.all_gather(sparse_desc, 'env', axis=1, tiled=True)  76.3 us
    another operation x6, other arithmetic, shards(): lower_factor = jnp.linalg.cholesky(gram_matrix)  37.4 us
    dot_general x7, matrix products, one_group(): return jnp.dot(weights, rows_window, precision=lax.Precision.HIGHEST)  26.1 us
    another operation x3, other arithmetic, shards(): jax.scipy.linalg.solve_triangular(lower_factor, panel_cols.T, lower=True)  22.7 us
  transfers between devices with their start and end apart: 4, of which 4 were waited for; matrix products, arithmetic and copies ran while one was open for 1% of the time, Pallas kernels for 0%

commit v1 on v0

v1 whole, which is shorter than its diff:
```python
import jax
import jax.numpy as jnp
from jax import lax
from jax.experimental import pallas as pl
from jax.experimental.pallas import tpu as pltpu
from jax.sharding import PartitionSpec as P

DESC = 1000
PANEL = 256
TILE = 256
N_Z = 16
N_SP = 16
CONF = 448
ENV = 1024
REG = 64
ROWS = CONF + REG
SLOTS = 5
COLS = SLOTS * PANEL
HALF = PANEL // 2
START = 0.95

cube_scale = 15.0 ** (-0.5)
dot_scale = DESC ** (-0.5)
VMEM_LIMIT = 60 * 1024 * 1024

SAME_CORE = [[2 * z + c for z in range(N_Z)] for c in range(2)]
CORE_SWAP = [(i, i ^ 1) for i in range(2 * N_Z)]


def nt(a, b):
    return lax.dot_general(a, b, (((1,), (1,)), ((), ())), preferred_element_type=jnp.float32)


def nn(a, b):
    return lax.dot_general(a, b, (((1,), (0,)), ((), ())), preferred_element_type=jnp.float32)


def halves(x):
    hi = x.astype(jnp.bfloat16)
    lo = (x - hi.astype(jnp.float32)).astype(jnp.bfloat16)
    return hi, lo


def cubed(product):
    scaled = product * dot_scale
    return scaled * scaled * scaled * cube_scale


def panel_kernel(points, env, reg, starts, finish, inverse, panel_ref, hi_ref, lo_ref, gram_ref, member_ref):
    position = lax.broadcasted_iota(jnp.int32, (CONF, ENV), 1)
    inside = (position >= starts[...]) & (position < finish[...])
    member = inside.astype(jnp.float32).astype(jnp.bfloat16)
    member_ref[...] = member
    pts = points[...]
    hi, lo = halves(cubed(nt(pts, env[...])))
    energy = (nt(hi, member) + nt(lo, member)) * inverse[...]
    panel_t = jnp.concatenate([energy, cubed(nt(pts, reg[...]))], 1)
    panel_ref[...] = panel_t.T
    hi, lo = halves(panel_t)
    hi_ref[...] = hi
    lo_ref[...] = lo
    gram_ref[...] = lax.dot_general(
        panel_t,
        panel_t,
        (((1,), (1,)), ((), ())),
        precision=lax.Precision.HIGHEST,
        preferred_element_type=jnp.float32,
    )


def panel_step(points, env, reg, starts, finish, inverse):
    return pl.pallas_call(
        panel_kernel,
        out_shape=(
            jax.ShapeDtypeStruct((ROWS, PANEL), jnp.float32),
            jax.ShapeDtypeStruct((PANEL, ROWS), jnp.bfloat16),
            jax.ShapeDtypeStruct((PANEL, ROWS), jnp.bfloat16),
            jax.ShapeDtypeStruct((PANEL, PANEL), jnp.float32),
            jax.ShapeDtypeStruct((CONF, ENV), jnp.bfloat16),
        ),
        compiler_params=pltpu.CompilerParams(vmem_limit_bytes=VMEM_LIMIT),
        name="panel",
    )(points, env, reg, starts, finish, inverse)


def design_kernel(core, points, env, reg, member, inverse, panel_hi, panel_lo, design_ref, keep_ref, send_ref):
    pts = points[...]
    hi, lo = halves(cubed(nt(env[...], pts)))
    weights = member[...]
    energy = (nn(weights, hi) + nn(weights, lo)) * inverse[...]
    rows = jnp.concatenate([energy, cubed(nt(reg[...], pts))], 0)
    design_ref[...] = rows
    hi, lo = halves(rows)
    left = panel_hi[...]
    product = nn(left, hi) + nn(left, lo) + nn(panel_lo[...], hi)

    @pl.when(core[0] == 0)
    def _():
        keep_ref[...] = product[:HALF]
        send_ref[...] = product[HALF:]

    @pl.when(core[0] != 0)
    def _():
        keep_ref[...] = product[HALF:]
        send_ref[...] = product[:HALF]


def design_step(core, points, env, reg, member, inverse, panel_hi, panel_lo):
    vmem = pl.BlockSpec(memory_space=pltpu.VMEM)
    return pl.pallas_call(
        design_kernel,
        in_specs=[pl.BlockSpec(memory_space=pltpu.SMEM)] + [vmem] * 7,
        out_specs=(vmem, vmem, vmem),
        out_shape=(
            jax.ShapeDtypeStruct((ROWS, COLS), jnp.float32),
            jax.ShapeDtypeStruct((HALF, COLS), jnp.float32),
            jax.ShapeDtypeStruct((HALF, COLS), jnp.float32),
        ),
        compiler_params=pltpu.CompilerParams(vmem_limit_bytes=VMEM_LIMIT),
        cost_estimate=pl.CostEstimate(flops=7 * 10**9, bytes_accessed=9 * 10**6, transcendentals=0),
        name="design",
    )(core, points, env, reg, member, inverse, panel_hi, panel_lo)


FULL = dict(precision=lax.Precision.HIGHEST, preferred_element_type=jnp.float32)


def stacked(core, own, other):
    return jnp.where(core == 0, jnp.concatenate([own, other], 0), jnp.concatenate([other, own], 0))


def factor_kernel(core, own, other, inv_ref, x_ref, s_ref):
    row = lax.broadcasted_iota(jnp.int32, (PANEL, PANEL), 0)
    col = lax.broadcasted_iota(jnp.int32, (PANEL, PANEL), 1)
    diag = (row == col).astype(jnp.float32)
    phi = jnp.where(row > col, 1.0, 0.5 * diag)
    g = stacked(core[0], own[...], other[...])
    on_diag = g * diag
    d_row = lax.rsqrt(jnp.sum(on_diag, 0, keepdims=True))
    d_col = lax.rsqrt(jnp.sum(on_diag, 1, keepdims=True))
    scaled = g * d_row * d_col
    x = START * (diag - phi * (START * START * scaled - diag))
    low = scaled.astype(jnp.bfloat16)
    for _ in range(2):
        x_low = x.astype(jnp.bfloat16)
        error = nt(nn(x_low, low).astype(jnp.bfloat16), x_low) - diag
        x = x - nn((phi * error).astype(jnp.bfloat16), x_low)
    x_ref[...] = x
    s_ref[...] = scaled

    def more(state):
        step, size = state
        return (step < 12) & (size >= 1e-6) & (size < 1e6)

    def refine(state):
        x = x_ref[...]
        half = lax.dot_general(x, s_ref[...], (((1,), (0,)), ((), ())), **FULL)
        error = lax.dot_general(half, x, (((1,), (1,)), ((), ())), **FULL) - diag
        x_ref[...] = x - nn((phi * error).astype(jnp.bfloat16), x.astype(jnp.bfloat16))
        return state[0] + 1, jnp.sum(error * error)

    _, size = lax.while_loop(more, refine, (0, jnp.float32(1.0)))
    inv_ref[...] = x_ref[...] * d_row

    @pl.when(jnp.logical_not(size < 1e-6))
    def _():
        x_ref[...] = diag
        s_ref[...] = scaled
        index = lax.broadcasted_iota(jnp.int32, (PANEL, 1), 0)
        lane = lax.broadcasted_iota(jnp.int32, (1, PANEL), 1)

        def eliminate(j, carry):
            s = s_ref[...]
            s_row = s_ref[pl.ds(j, 1), :]
            x_row = x_ref[pl.ds(j, 1), :]
            pivot = jnp.sum(jnp.where(lane == j, s_row, 0.0), 1, keepdims=True)
            column = jnp.sum(jnp.where(lane == j, s, 0.0), 1, keepdims=True)
            below = jnp.where(index > j, column / pivot, 0.0)
            s_ref[...] = s - below * s_row
            x = x_ref[...] - below * x_row
            x_ref[...] = jnp.where(index == j, x * lax.rsqrt(pivot), x)
            return carry

        lax.fori_loop(0, PANEL, eliminate, 0)
        inv_ref[...] = x_ref[...] * d_row


def factor_step(core, own, other):
    vmem = pl.BlockSpec(memory_space=pltpu.VMEM)
    return pl.pallas_call(
        factor_kernel,
        in_specs=[pl.BlockSpec(memory_space=pltpu.SMEM), vmem, vmem],
        out_specs=vmem,
        out_shape=jax.ShapeDtypeStruct((PANEL, PANEL), jnp.float32),
        scratch_shapes=[pltpu.VMEM((PANEL, PANEL), jnp.float32)] * 2,
        compiler_params=pltpu.CompilerParams(vmem_limit_bytes=VMEM_LIMIT),
        name="factor",
    )(core, own, other)


def update_kernel(slot, design, own, other, inverse_factor, panel, updated_ref, coupling_ref, q_ref):
    t = pl.program_id(0)

    @pl.when(t == 0)
    def _():
        p_hi, p_lo = halves(panel[...])
        f_hi, f_lo = halves(inverse_factor[...])
        q_ref[...] = nt(p_hi, f_hi) + nt(p_hi, f_lo) + nt(p_lo, f_hi)

    @pl.when(t < slot[0])
    def _():
        updated_ref[...] = design[...]
        coupling_ref[...] = jnp.zeros((PANEL, TILE), jnp.float32)

    @pl.when(t >= slot[0])
    def _():
        f_hi, f_lo = halves(inverse_factor[...])
        w_hi, w_lo = halves(stacked(slot[1], own[...], other[...]))
        coupling = nn(f_hi, w_hi) + nn(f_hi, w_lo) + nn(f_lo, w_hi)
        coupling_ref[...] = coupling
        q_hi, q_lo = halves(q_ref[...])
        c_hi, c_lo = halves(coupling)
        updated_ref[...] = design[...] - (nn(q_hi, c_hi) + nn(q_hi, c_lo) + nn(q_lo, c_hi))

    @pl.when(t == slot[0])
    def _():
        updated_ref[...] = q_ref[...]


def update_step(slot, design, own, other, inverse_factor, panel):
    return pl.pallas_call(
        update_kernel,
        grid_spec=pltpu.PrefetchScalarGridSpec(
            num_scalar_prefetch=1,
            grid=(SLOTS,),
            in_specs=[
                pl.BlockSpec((ROWS, TILE), lambda t, s: (0, t)),
                pl.BlockSpec((HALF, TILE), lambda t, s: (0, t)),
                pl.BlockSpec((HALF, TILE), lambda t, s: (0, t)),
                pl.BlockSpec((PANEL, PANEL), lambda t, s: (0, 0)),
                pl.BlockSpec((ROWS, PANEL), lambda t, s: (0, 0)),
            ],
            out_specs=(
                pl.BlockSpec((ROWS, TILE), lambda t, s: (0, t)),
                pl.BlockSpec((PANEL, TILE), lambda t, s: (0, t)),
            ),
            scratch_shapes=[pltpu.VMEM((ROWS, PANEL), jnp.float32)],
        ),
        out_shape=(
            jax.ShapeDtypeStruct((ROWS, COLS), jnp.float32),
            jax.ShapeDtypeStruct((PANEL, COLS), jnp.float32),
        ),
        compiler_params=pltpu.CompilerParams(vmem_limit_bytes=VMEM_LIMIT),
        name="update",
    )(slot, design, own, other, inverse_factor, panel)


def shards(env_desc, env_counts, reg_desc, sparse_desc, panel_block):
    core = lax.axis_index("env") % 2
    column_shard = lax.axis_index("sp")
    owner = panel_block // SLOTS

    gathered = lax.all_gather(sparse_desc, "env", axis=1, tiled=True)

    with jax.named_scope("panel_points"):
        mine = lax.dynamic_index_in_dim(sparse_desc, panel_block - owner * SLOTS, 0, keepdims=False)
        offered = jnp.broadcast_to(mine[None], (N_SP,) + mine.shape)
        offered = lax.all_to_all(offered, "sp", 0, 0)
        mine = lax.dynamic_index_in_dim(offered, owner, 0, keepdims=False)
        panel_points = lax.all_gather(mine, "env", axis=0, tiled=True)

    counts = env_counts[0]
    finish = jnp.cumsum(counts)
    starts = finish - counts
    inverse = 1.0 / counts.astype(jnp.float32)
    panel, panel_hi, panel_lo, gram, member = panel_step(
        panel_points, env_desc, reg_desc, starts[:, None], finish[:, None], inverse[None, :]
    )

    with jax.named_scope("gram"):
        pieces = gram.reshape(2, N_Z, HALF // N_Z, PANEL).swapaxes(0, 1)
        pieces = pieces.reshape(2 * N_Z, HALF // N_Z, PANEL)
        gram_rows = jnp.sum(lax.all_to_all(pieces, "env", 0, 0), 0)

    core_index = core.reshape(1).astype(jnp.int32)
    points = gathered.reshape(COLS, DESC)
    design, keep, send = design_step(
        core_index, points, env_desc, reg_desc, member, inverse[:, None], panel_hi, panel_lo
    )

    with jax.named_scope("product"):
        send, gram_rows = lax.optimization_barrier((send, gram_rows))
        keep = keep + lax.ppermute(send, "env", CORE_SWAP)
        keep = keep.reshape(N_Z, HALF // N_Z, COLS)
        keep = lax.all_to_all(keep, "env", 0, 0, axis_index_groups=SAME_CORE)
        rows = jnp.concatenate([jnp.sum(keep, 0), gram_rows], 1)
        own = lax.all_gather(rows, "env", axis=0, tiled=True, axis_index_groups=SAME_CORE)
        own_gram, own = own[:, COLS:], own[:, :COLS]
        other_gram = lax.ppermute(own_gram, "env", CORE_SWAP)
        other = lax.ppermute(own, "env", CORE_SWAP)

    inverse_factor = factor_step(core_index, own_gram, other_gram)
    slot = jnp.stack([panel_block - column_shard * SLOTS, core]).astype(jnp.int32)
    return update_step(slot, design, own, other, inverse_factor, panel)


def solution(mesh):
    in_specs = (P("env", None), P("env", None), P("env", None), P("sp", "env", None), P())
    out_specs = (P("env", "sp"), P(None, "sp"))
    return jax.shard_map(shards, mesh=mesh, in_specs=in_specs, out_specs=out_specs, check_vma=False)
```

time: 764 us -> 266 us (0.35)
  waiting for transfers between devices: 607 us -> 24.2 us
  blocking collectives: 0 us -> 106 us
  Pallas kernels: 0 us -> 72.3 us
  other arithmetic: 68.4 us -> 3.59 us
  matrix products: 53.8 us -> 0 us
  starting transfers between devices: 0.34 us -> 31.6 us
    psum x3 -> x0, waiting for transfers between devices: 530 us -> none  [the longest x1 212 us: shards(): coupling = lax.psum(cross_gram(orthogonal, design), 'env')]
    all_gather x1, waiting for transfers between devices: 76.3 us -> 0.02 us  [shards(): gathered = lax.all_gather(sparse_desc, 'env', axis=1, tiled=True)]
    pallas_call x0 -> x4, Pallas kernels: none -> 72.3 us  [the longest x1 47.1 us: factor_step(): pl.pallas_call(factor_kernel, in_specs=[pl.BlockSpec(memory_space=pltpu.S...]
    all_gather x0 -> x2, blocking collectives: none -> 68.7 us  [the longest x1 42.1 us: shards(): panel_points = lax.all_gather(mine, 'env', axis=0, tiled=True)]
    another operation x13 -> x5, other arithmetic: 60.5 us -> 1.77 us  [the longest x6 37.4 us: shards(): lower_factor = jnp.linalg.cholesky(gram_matrix)]
    dot_general x12 -> x0, matrix products: 47.3 us -> none  [the longest x7 26.1 us: one_group(): return jnp.dot(weights, rows_window, precision=lax.Precision.HIGHEST)]
    all_to_all x0 -> x1, blocking collectives: none -> 37.5 us  [shards(): keep = lax.all_to_all(keep, 'env', 0, 0, axis_index_groups=SAME_CORE)]
    all_to_all x0 -> x2, waiting for transfers between devices: none -> 21.2 us  [the longest x1 21.2 us: shards(): gram_rows = jnp.sum(lax.all_to_all(pieces, 'env', 0, 0), 0)]
  transfers between devices with their start and end apart: 4 -> 6, of which waited for: 4 -> 3; matrix products, arithmetic and copies ran while one was open for 1% -> 5% of each run, Pallas kernels for 0% -> 20%
where the time goes in v1:
time: 266 us; the launch traced here: 265 us
  blocking collectives  106 us (40%)
  Pallas kernels  72.3 us (27%)
  starting transfers between devices  31.6 us (12%)
  waiting for transfers between devices  24.2 us (9%)
  between operations  14.8 us (6%)
  local copies, waits for them, and re-layouts  12 us (5%)
  other arithmetic  3.59 us (1%)
    pallas_call x1, Pallas kernels, factor_step(): pl.pallas_call(factor_kernel, in_specs=[pl.BlockSpec(memory_space=pltpu.S...  47.1 us
    all_gather x1, blocking collectives, shards(): panel_points = lax.all_gather(mine, 'env', axis=0, tiled=True)  42.1 us
    all_to_all x1, blocking collectives, shards(): keep = lax.all_to_all(keep, 'env', 0, 0, axis_index_groups=SAME_CORE)  37.5 us
    all_gather x1, blocking collectives, shards(): lax.all_gather(rows, 'env', axis=0, tiled=True, axis_index_groups=SAME_CORE)  26.6 us
    all_to_all x1, waiting for transfers between devices, shards(): gram_rows = jnp.sum(lax.all_to_all(pieces, 'env', 0, 0), 0)  21.2 us
    pallas_call x1, Pallas kernels, design_step(): pl.pallas_call(design_kernel, in_specs=[pl.BlockSpec(memory_space=pltpu.S...  12.5 us
    ppermute x1, starting transfers between devices, shards(): other = lax.ppermute(own, 'env', CORE_SWAP)  11.6 us
    all_to_all x1, starting transfers between devices, shards(): offered = lax.all_to_all(offered, 'sp', 0, 0)  7.72 us
  transfers between devices with their start and end apart: 6, of which 3 were waited for; matrix products, arithmetic and copies ran while one was open for 5% of the time, Pallas kernels for 20%

profile of v1, /device:TPU:1, one launch (start us, length us, event | category | flops | bytes accessed | tf_op | source)
XLA Modules:
  0.0 264.7 jit_solution(7638000875555979529)
XLA Ops:
  7.2 0.7 all-gather.3.cloned.1.call-update
  8.6 0.7 dynamic-slice_bitcast_fusion
  9.3 0.7 broadcast_in_dim.17
  10.0 7.7 %all-to-all-start = ((bf16[16,8,1000]{2,1,0:T(8,128)(2,1)}), bf16[16,8,1000]{2,1,0:T(8,128)(2,1)S(1)}, u32[]{:S(2)}, u32[]{:S(2)}) async-start(bf16[16,8,1000]{2,1,0:T(8,128)(2,1)} %broadcast_in_dim.17), calls=%async_computation | async-start | bytes 524288 | tf_op jit(solution)/shard_map/panel_points/all_to_all | solution.py:268
  17.8 0.7 pad_bitcast_fusion
  18.4 0.3 reduce-window.9
  18.9 0.1 slice_reduce_fusion
  19.1 0.7 fusion
  19.7 0.8 copy.10.starts
  20.6 0.8 copy.11.finish
  21.4 3.9 %copy.12.env = bf16[1024,1000]{1,0:T(8,128)(2,1)} copy(bf16[1024,1000]{0,1:T(8,128)(2,1)} %param.5) | data formatting | bytes 4096000 | tf_op args[0]
  25.3 0.6 convert_divide_fusion.inverse
  25.9 42.1 %all-gather = bf16[1,256,1000]{2,1,0:T(8,128)(2,1)} all-gather(bf16[1,8,1000]{2,1,0:T(8,128)(2,1)S(1)} %constant_dynamic-slice_fusion), channel_id=2, replica_groups=mesh['env'=32,'sp'=16] {'env'}, dimensions={1}, use_global_device_ids=true | all-gather | bytes 528000 | tf_op jit(solution)/shard_map/panel_points/all_gather | solution.py:270
  68.0 5.7 %panel.1 = (f32[512,256]{1,0:T(8,128)}, bf16[256,512]{1,0:T(8,128)(2,1)}, bf16[256,512]{1,0:T(8,128)(2,1)}, f32[256,256]{1,0:T(8,128)}, bf16[448,1024]{1,0:T(8,128)(2,1)}) custom-call(bf16[256,1000]{1,0:T(8,128)(2,1)} %bitcast.21, bf16[1024,1000]{1,0:T(8,128)(2,1)} %copy.12.env, bf16[64,1000]{1,0:T(8,128)(2,1)} %reg.3, s32[448,1]{1,0:T(8,128)} %copy.10.starts, ...), custom_call_target="tpu_custom_call" | custom-call | tf_op jit(solution)/shard_map/panel/pallas_call | solution.py:72
  73.7 1.7 copy.14
  75.4 7.2 %all-to-all-start.1 = ((f32[32,8,256]{2,1,0:T(8,128)}), f32[32,8,256]{2,1,0:T(8,128)S(1)}, u32[]{:S(2)}, u32[]{:S(2)}) async-start(f32[32,8,256]{2,1,0:T(8,128)} %bitcast.13), calls=%async_computation.1 | async-start | bytes 524288 | tf_op jit(solution)/shard_map/gram/all_to_all | solution.py:283
  82.6 0.8 copy.13.inverse
  83.4 21.2 %all-to-all-done.1 = f32[32,8,256]{2,1,0:T(8,128)S(1)} async-done(((f32[32,8,256]{2,1,0:T(8,128)}), f32[32,8,256]{2,1,0:T(8,128)S(1)}, u32[]{:S(2)}, u32[]{:S(2)}) %all-to-all-start.1) | async-done | bytes 262176 | tf_op jit(solution)/shard_map/gram/all_to_all | solution.py:283
  104.6 12.5 %design.1 = (f32[512,1280]{1,0:T(8,128)}, f32[128,1280]{1,0:T(8,128)}, f32[128,1280]{1,0:T(8,128)}) custom-call(s32[1]{0:T(128)} %bitcast.1.core, bf16[1280,1000]{1,0:T(8,128)(2,1)} %bitcast.27, bf16[1024,1000]{1,0:T(8,128)(2,1)} %copy.12.env, bf16[64,1000]{1,0:T(8,128)(2,1)} %reg.3, bf16[448,1024]{1,0:T(8,128)(2,1)} %get-tuple-element.12.member, ...), custom_call_target="tpu_custom_call" | custom-call | flops 7000000000 | bytes 9000000 | tf_op jit(solution)/shard_map/design/pallas_call | solution.py:110
  117.1 2.9 %collective-permute-start = (f32[128,1280]{1,0:T(8,128)}, f32[128,1280]{1,0:T(8,128)S(1)}, u32[]{:S(2)}, u32[]{:S(2)}) collective-permute-start(f32[128,1280]{1,0:T(8,128)} %get-tuple-element.19), channel_id=1, source_target_pairs={{0,16},{16,0},{32,48},{48,32},{64,80},{80,64},{96,112},{112,96},{1... | collective-permute-start | bytes 1966088 | tf_op jit(solution)/shard_map/product/ppermute | solution.py:293
  120.1 1.9 collective-permute-done
  122.0 1.2 add_bitcast_fusion
  123.1 37.5 %all_to_all.15 = f32[16,8,1280]{2,1,0:T(8,128)S(1)} all-to-all(f32[16,8,1280]{2,1,0:T(8,128)S(1)} %add_bitcast_fusion), channel_id=1, replica_groups={{0,32,64,96,128,160,192,224,256,288,320,352,384,416,448,480},{16,48,80,..., dimensions={0} | all-to-all | bytes 1310720 | tf_op jit(solution)/shard_map/product/all_to_all | solution.py:295
  160.7 26.6 %all_gather.11 = f32[128,1536]{1,0:T(8,128)S(1)} all-gather(f32[8,1536]{1,0:T(8,128)S(1)} %pad_maximum_fusion), channel_id=1, replica_groups={{0,32,64,96,128,160,192,224,256,288,320,352,384,416,448,480},{16,48,80,..., dimensions={0}, use_global_device_ids=true | all-gather | bytes 835584 | tf_op jit(solution)/shard_map/product/all_gather | solution.py:297
  187.4 11.6 %collective-permute-start.1 = (f32[128,1280]{1,0:T(8,128)S(1)}, f32[128,1280]{1,0:T(8,128)S(1)}, u32[]{:S(2)}, u32[]{:S(2)}) collective-permute-start(f32[128,1280]{1,0:T(8,128)S(1)} %slice.21.own), channel_id=1, source_target_pairs={{0,16},{16,0},{32,48},{48,32},{64,80},{80,64},{96,112},{112,96},{1... | collective-permute-start | bytes 1966088 | tf_op jit(solution)/shard_map/product/ppermute | solution.py:300
  199.0 2.1 collective-permute-start.2
  201.1 0.7 pad_add_fusion.slot
  201.8 0.5 collective-permute-done.2.other
  202.3 0.7 copy-done.3
  202.9 47.1 %factor.1.inverse_factor = f32[256,256]{1,0:T(8,128)} custom-call(s32[1]{0:T(128)} %bitcast.1.core, f32[128,256]{1,0:T(8,128)} %copy-done.2, f32[128,256]{1,0:T(8,128)} %copy-done.3), custom_call_target="tpu_custom_call" | custom-call | tf_op jit(solution)/shard_map/factor/pallas_call | solution.py:190
  250.0 0.8 copy-done.1
  250.8 7.1 %update.1 = (f32[512,1280]{1,0:T(8,128)}, f32[256,1280]{1,0:T(8,128)}) custom-call(s32[2]{0:T(128)} %pad_add_fusion.slot, f32[512,1280]{1,0:T(8,128)} %get-tuple-element.15.design, f32[128,1280]{1,0:T(8,128)} %copy-done, f32[128,1280]{1,0:T(8,128)} %copy-done.1, f32[256,256]{1,0:T(8,128)} %factor.1.inverse_factor, f32[512,256]{1,0:T(8,128)} %get-tuple-element.21.panel), custom_call_target="tpu_custom_call" | custom-call | tf_op jit(solution)/shard_map/update/pallas_call | solution.py:231
  (22 shorter events, 0.4 us)
Async XLA Ops:
  7.2 97.5 %all-gather.3.cloned.1.call-start = ((), (), s32[]{:S(2)}) async-start(), calls=%async_computation.3 | async-start | bytes 2703360 | tf_op jit(solution)/shard_map/all_gather | solution.py:263
  10.0 15.3 %copy-start.4 = (s32[1,448]{1,0:T(1,128)S(1)}, s32[1,448]{1,0:T(1,128)}, u32[]{:S(2)}) copy-start(s32[1,448]{1,0:T(1,128)} %param.6) | copy-start | bytes 5380
  10.0 15.9 %all-to-all-start = ((bf16[16,8,1000]{2,1,0:T(8,128)(2,1)}), bf16[16,8,1000]{2,1,0:T(8,128)(2,1)S(1)}, u32[]{:S(2)}, u32[]{:S(2)}) async-start(bf16[16,8,1000]{2,1,0:T(8,128)(2,1)} %broadcast_in_dim.17), calls=%async_computation | async-start | bytes 524288 | tf_op jit(solution)/shard_map/panel_points/all_to_all | solution.py:268
  75.4 29.2 %all-to-all-start.1 = ((f32[32,8,256]{2,1,0:T(8,128)}), f32[32,8,256]{2,1,0:T(8,128)S(1)}, u32[]{:S(2)}, u32[]{:S(2)}) async-start(f32[32,8,256]{2,1,0:T(8,128)} %bitcast.13), calls=%async_computation.1 | async-start | bytes 524288 | tf_op jit(solution)/shard_map/gram/all_to_all | solution.py:283
  117.1 4.9 %collective-permute-start = (f32[128,1280]{1,0:T(8,128)}, f32[128,1280]{1,0:T(8,128)S(1)}, u32[]{:S(2)}, u32[]{:S(2)}) collective-permute-start(f32[128,1280]{1,0:T(8,128)} %get-tuple-element.19), channel_id=1, source_target_pairs={{0,16},{16,0},{32,48},{48,32},{64,80},{80,64},{96,112},{112,96},{1... | collective-permute-start | bytes 1966088 | tf_op jit(solution)/shard_map/product/ppermute | solution.py:293
  187.4 62.6 %copy-start = (f32[128,1280]{1,0:T(8,128)}, f32[128,1280]{1,0:T(8,128)S(1)}, u32[]{:S(2)}) copy-start(f32[128,1280]{1,0:T(8,128)S(1)} %slice.21.own) | copy-start | bytes 1966084
  187.4 62.6 %collective-permute-start.1 = (f32[128,1280]{1,0:T(8,128)S(1)}, f32[128,1280]{1,0:T(8,128)S(1)}, u32[]{:S(2)}, u32[]{:S(2)}) collective-permute-start(f32[128,1280]{1,0:T(8,128)S(1)} %slice.21.own), channel_id=1, source_target_pairs={{0,16},{16,0},{32,48},{48,32},{64,80},{80,64},{96,112},{112,96},{1... | collective-permute-start | bytes 1966088 | tf_op jit(solution)/shard_map/product/ppermute | solution.py:300
  199.0 3.3 %copy-start.2 = (f32[128,256]{1,0:T(8,128)}, f32[128,256]{1,0:T(8,128)S(1)}, u32[]{:S(2)}) copy-start(f32[128,256]{1,0:T(8,128)S(1)} %slice.22.own) | copy-start | bytes 393220
  199.0 3.2 %collective-permute-start.2 = (f32[128,256]{1,0:T(8,128)S(1)}, f32[128,256]{1,0:T(8,128)S(1)}, u32[]{:S(2)}, u32[]{:S(2)}) collective-permute-start(f32[128,256]{1,0:T(8,128)S(1)} %slice.22.own), channel_id=1, source_target_pairs={{0,16},{16,0},{32,48},{48,32},{64,80},{80,64},{96,112},{112,96},{1... | collective-permute-start | bytes 393224 | tf_op jit(solution)/shard_map/product/ppermute | solution.py:299
  202.3 0.7 copy-start.3
  250.0 0.8 copy-start.1
Sparse Core Ops, SparseCore 0:
  10.1 79.2 all-gather.2

commit v2 on v1

--- a/solution.py
+++ b/solution.py
@@ -21,7 +21,8 @@
 
 cube_scale = 15.0 ** (-0.5)
 dot_scale = DESC ** (-0.5)
-VMEM_LIMIT = 60 * 1024 * 1024
+VMEM_LIMIT = 40 * 1024 * 1024
+DESIGN_VMEM = 60 * 1024 * 1024
 
 SAME_CORE = [[2 * z + c for z in range(N_Z)] for c in range(2)]
 CORE_SWAP = [(i, i ^ 1) for i in range(2 * N_Z)]
@@ -83,43 +84,46 @@
     )(points, env, reg, starts, finish, inverse)
 
 
-def design_kernel(core, points, env, reg, member, inverse, panel_hi, panel_lo, design_ref, keep_ref, send_ref):
+def design_kernel(
+    place, points, env, reg, member, inverse, panel_hi, panel_lo, design_ref, keep_ref, send_ref, rows_ref, sem
+):
     pts = points[...]
     hi, lo = halves(cubed(nt(env[...], pts)))
     weights = member[...]
-    energy = (nn(weights, hi) + nn(weights, lo)) * inverse[...]
-    rows = jnp.concatenate([energy, cubed(nt(reg[...], pts))], 0)
-    design_ref[...] = rows
-    hi, lo = halves(rows)
+    rows_ref[:CONF] = (nn(weights, hi) + nn(weights, lo)) * inverse[...]
+    rows_ref[CONF:] = cubed(nt(reg[...], pts))
+    leave = pltpu.make_async_copy(rows_ref, design_ref, sem)
+    leave.start()
+    hi, lo = halves(rows_ref[...])
     left = panel_hi[...]
     product = nn(left, hi) + nn(left, lo) + nn(panel_lo[...], hi)
-
-    @pl.when(core[0] == 0)
-    def _():
-        keep_ref[...] = product[:HALF]
-        send_ref[...] = product[HALF:]
-
-    @pl.when(core[0] != 0)
-    def _():
-        keep_ref[...] = product[HALF:]
-        send_ref[...] = product[:HALF]
-
-
-def design_step(core, points, env, reg, member, inverse, panel_hi, panel_lo):
-    vmem = pl.BlockSpec(memory_space=pltpu.VMEM)
+    first = place[0] == 0
+    keep_ref[...] = jnp.where(first, product[:HALF], product[HALF:])
+    send_ref[...] = jnp.where(first, product[HALF:], product[:HALF])
+    leave.wait()
+
+
+def design_step(place, points, env, reg, member, inverse, panel_hi, panel_lo):
+    half = pl.BlockSpec((HALF, COLS), lambda t, s: (0, 0))
+    arrays = (points, env, reg, member, inverse, panel_hi, panel_lo)
     return pl.pallas_call(
         design_kernel,
-        in_specs=[pl.BlockSpec(memory_space=pltpu.SMEM)] + [vmem] * 7,
-        out_specs=(vmem, vmem, vmem),
+        grid_spec=pltpu.PrefetchScalarGridSpec(
+            num_scalar_prefetch=1,
+            grid=(1,),
+            in_specs=[pl.BlockSpec(a.shape, lambda t, s: (0, 0)) for a in arrays],
+            out_specs=(pl.BlockSpec(memory_space=pl.ANY), half, half),
+            scratch_shapes=[pltpu.VMEM((ROWS, COLS), jnp.float32), pltpu.SemaphoreType.DMA],
+        ),
         out_shape=(
             jax.ShapeDtypeStruct((ROWS, COLS), jnp.float32),
             jax.ShapeDtypeStruct((HALF, COLS), jnp.float32),
             jax.ShapeDtypeStruct((HALF, COLS), jnp.float32),
         ),
-        compiler_params=pltpu.CompilerParams(vmem_limit_bytes=VMEM_LIMIT),
+        compiler_params=pltpu.CompilerParams(vmem_limit_bytes=DESIGN_VMEM),
         cost_estimate=pl.CostEstimate(flops=7 * 10**9, bytes_accessed=9 * 10**6, transcendentals=0),
         name="design",
-    )(core, points, env, reg, member, inverse, panel_hi, panel_lo)
+    )(place, *arrays)
 
 
 FULL = dict(precision=lax.Precision.HIGHEST, preferred_element_type=jnp.float32)
@@ -185,20 +189,24 @@
         inv_ref[...] = x_ref[...] * d_row
 
 
-def factor_step(core, own, other):
-    vmem = pl.BlockSpec(memory_space=pltpu.VMEM)
+def factor_step(place, own, other):
+    columns = pl.BlockSpec((HALF, PANEL), lambda t, s: (0, SLOTS))
     return pl.pallas_call(
         factor_kernel,
-        in_specs=[pl.BlockSpec(memory_space=pltpu.SMEM), vmem, vmem],
-        out_specs=vmem,
+        grid_spec=pltpu.PrefetchScalarGridSpec(
+            num_scalar_prefetch=1,
+            grid=(1,),
+            in_specs=[columns, columns],
+            out_specs=pl.BlockSpec((PANEL, PANEL), lambda t, s: (0, 0)),
+            scratch_shapes=[pltpu.VMEM((PANEL, PANEL), jnp.float32)] * 2,
+        ),
         out_shape=jax.ShapeDtypeStruct((PANEL, PANEL), jnp.float32),
-        scratch_shapes=[pltpu.VMEM((PANEL, PANEL), jnp.float32)] * 2,
         compiler_params=pltpu.CompilerParams(vmem_limit_bytes=VMEM_LIMIT),
         name="factor",
-    )(core, own, other)
-
-
-def update_kernel(slot, design, own, other, inverse_factor, panel, updated_ref, coupling_ref, q_ref):
+    )(place, own, other)
+
+
+def update_kernel(place, design, own, other, inverse_factor, panel, updated_ref, coupling_ref, q_ref):
     t = pl.program_id(0)
 
     @pl.when(t == 0)
@@ -207,27 +215,27 @@
         f_hi, f_lo = halves(inverse_factor[...])
         q_ref[...] = nt(p_hi, f_hi) + nt(p_hi, f_lo) + nt(p_lo, f_hi)
 
-    @pl.when(t < slot[0])
+    @pl.when(t < place[1])
     def _():
         updated_ref[...] = design[...]
         coupling_ref[...] = jnp.zeros((PANEL, TILE), jnp.float32)
 
-    @pl.when(t >= slot[0])
+    @pl.when(t >= place[1])
     def _():
         f_hi, f_lo = halves(inverse_factor[...])
-        w_hi, w_lo = halves(stacked(slot[1], own[...], other[...]))
+        w_hi, w_lo = halves(stacked(place[0], own[...], other[...]))
         coupling = nn(f_hi, w_hi) + nn(f_hi, w_lo) + nn(f_lo, w_hi)
         coupling_ref[...] = coupling
         q_hi, q_lo = halves(q_ref[...])
         c_hi, c_lo = halves(coupling)
         updated_ref[...] = design[...] - (nn(q_hi, c_hi) + nn(q_hi, c_lo) + nn(q_lo, c_hi))
 
-    @pl.when(t == slot[0])
+    @pl.when(t == place[1])
     def _():
         updated_ref[...] = q_ref[...]
 
 
-def update_step(slot, design, own, other, inverse_factor, panel):
+def update_step(place, design, own, other, inverse_factor, panel):
     return pl.pallas_call(
         update_kernel,
         grid_spec=pltpu.PrefetchScalarGridSpec(
@@ -252,7 +260,7 @@
         ),
         compiler_params=pltpu.CompilerParams(vmem_limit_bytes=VMEM_LIMIT),
         name="update",
-    )(slot, design, own, other, inverse_factor, panel)
+    )(place, design, own, other, inverse_factor, panel)
 
 
 def shards(env_desc, env_counts, reg_desc, sparse_desc, panel_block):
@@ -273,6 +281,7 @@
     finish = jnp.cumsum(counts)
     starts = finish - counts
     inverse = 1.0 / counts.astype(jnp.float32)
+    place = jnp.stack([core, panel_block - column_shard * SLOTS]).astype(jnp.int32)
     panel, panel_hi, panel_lo, gram, member = panel_step(
         panel_points, env_desc, reg_desc, starts[:, None], finish[:, None], inverse[None, :]
     )
@@ -280,28 +289,24 @@
     with jax.named_scope("gram"):
         pieces = gram.reshape(2, N_Z, HALF // N_Z, PANEL).swapaxes(0, 1)
         pieces = pieces.reshape(2 * N_Z, HALF // N_Z, PANEL)
-        gram_rows = jnp.sum(lax.all_to_all(pieces, "env", 0, 0), 0)
-
-    core_index = core.reshape(1).astype(jnp.int32)
+        pieces = lax.all_to_all(pieces, "env", 0, 0)
+
     points = gathered.reshape(COLS, DESC)
     design, keep, send = design_step(
-        core_index, points, env_desc, reg_desc, member, inverse[:, None], panel_hi, panel_lo
+        place, points, env_desc, reg_desc, member, inverse[:, None], panel_hi, panel_lo
     )
 
     with jax.named_scope("product"):
-        send, gram_rows = lax.optimization_barrier((send, gram_rows))
+        send, pieces = lax.optimization_barrier((send, pieces))
         keep = keep + lax.ppermute(send, "env", CORE_SWAP)
         keep = keep.reshape(N_Z, HALF // N_Z, COLS)
         keep = lax.all_to_all(keep, "env", 0, 0, axis_index_groups=SAME_CORE)
-        rows = jnp.concatenate([jnp.sum(keep, 0), gram_rows], 1)
+        rows = jnp.concatenate([jnp.sum(keep, 0), jnp.sum(pieces, 0)], 1)
         own = lax.all_gather(rows, "env", axis=0, tiled=True, axis_index_groups=SAME_CORE)
-        own_gram, own = own[:, COLS:], own[:, :COLS]
-        other_gram = lax.ppermute(own_gram, "env", CORE_SWAP)
         other = lax.ppermute(own, "env", CORE_SWAP)
 
-    inverse_factor = factor_step(core_index, own_gram, other_gram)
-    slot = jnp.stack([panel_block - column_shard * SLOTS, core]).astype(jnp.int32)
-    return update_step(slot, design, own, other, inverse_factor, panel)
+    inverse_factor = factor_step(place, own, other)
+    return update_step(place, design, own, other, inverse_factor, panel)
 
 
 def solution(mesh):

time: 266 us -> 254 us (0.955)
  blocking collectives: 106 us -> 69.6 us
  waiting for transfers between devices: 24.2 us -> 50 us
  Pallas kernels: 72.3 us -> 65.4 us
  starting transfers between devices: 31.6 us -> 37.9 us
  local copies, waits for them, and re-layouts: 12 us -> 8.18 us
    all_to_all x1 -> x0, blocking collectives: 37.5 us -> none  [shards(): keep = lax.all_to_all(keep, 'env', 0, 0, axis_index_groups=SAME_CORE)]
    all_gather x1, waiting for transfers between devices: 0.02 us -> 14.4 us  [shards(): gathered = lax.all_gather(sparse_desc, 'env', axis=1, tiled=True)]
    all_to_all x1 -> x2, waiting for transfers between devices: 21.2 us -> 29 us  [the longest x1 29 us: shards(): keep = lax.all_to_all(keep, 'env', 0, 0, axis_index_groups=SAME_CORE)]
    all_to_all x1 -> x2, starting transfers between devices: 7.16 us -> 14.7 us  [the longest x1 7.66 us: shards(): keep = lax.all_to_all(keep, 'env', 0, 0, axis_index_groups=SAME_CORE)]
    all_gather x1, blocking collectives: 26.6 us -> 29.8 us  [shards(): lax.all_gather(rows, 'env', axis=0, tiled=True, axis_index_groups=SAME_CORE)]
    pallas_call x1, Pallas kernels: 7.06 us -> 4 us  [update_step(): pl.pallas_call(update_kernel, grid_spec=pltpu.PrefetchScalarGridSpec(num_...]
    pallas_call x1, Pallas kernels: 5.71 us -> 2.74 us  [panel_step(): pl.pallas_call(panel_kernel, out_shape=(jax.ShapeDtypeStruct((ROWS, PANEL...]
    unnamed x11 -> x17, local copies, waits for them, and re-layouts: 5.42 us -> 3.92 us
  transfers between devices with their start and end apart: 6 -> 6, of which waited for: 3 -> 5; matrix products, arithmetic and copies ran while one was open for 5% -> 4% of each run, Pallas kernels for 20% -> 6%
where the time goes in v2:
time: 254 us; the launch traced here: 251 us
  blocking collectives  69.6 us (27%)
  Pallas kernels  65.4 us (26%)
  waiting for transfers between devices  50 us (20%)
  starting transfers between devices  37.9 us (15%)
  between operations  14.9 us (6%)
  local copies, waits for them, and re-layouts  8.18 us (3%)
  other arithmetic  4.92 us (2%)
    pallas_call x1, Pallas kernels, factor_step(): pl.pallas_call(factor_kernel, grid_spec=pltpu.PrefetchScalarGridSpec(num_...  45.9 us
    all_gather x1, blocking collectives, shards(): panel_points = lax.all_gather(mine, 'env', axis=0, tiled=True)  39.8 us
    all_gather x1, blocking collectives, shards(): lax.all_gather(rows, 'env', axis=0, tiled=True, axis_index_groups=SAME_CORE)  29.8 us
    all_to_all x1, waiting for transfers between devices, shards(): keep = lax.all_to_all(keep, 'env', 0, 0, axis_index_groups=SAME_CORE)  29 us
    all_gather x1, waiting for transfers between devices, shards(): gathered = lax.all_gather(sparse_desc, 'env', axis=1, tiled=True)  14.4 us
    ppermute x1, starting transfers between devices, shards(): other = lax.ppermute(own, 'env', CORE_SWAP)  13.3 us
    pallas_call x1, Pallas kernels, design_step(): pl.pallas_call(design_kernel, grid_spec=pltpu.PrefetchScalarGridSpec(num_...  12.7 us
    all_to_all x1, starting transfers between devices, shards(): offered = lax.all_to_all(offered, 'sp', 0, 0)  7.72 us
  transfers between devices with their start and end apart: 6, of which 5 were waited for; matrix products, arithmetic and copies ran while one was open for 4% of the time, Pallas kernels for 6%

profile of v2, /device:TPU:1, one launch (start us, length us, event | category | flops | bytes accessed | tf_op | source)
XLA Modules:
  0.0 250.9 jit_solution(14304731240963788790)
XLA Ops:
  7.2 0.7 all-gather.3.cloned.1.call-update
  8.6 0.7 dynamic-slice_bitcast_fusion
  9.3 0.7 broadcast_in_dim.17
  10.0 7.7 %all-to-all-start = ((bf16[16,8,1000]{2,1,0:T(8,128)(2,1)}), bf16[16,8,1000]{2,1,0:T(8,128)(2,1)S(1)}, u32[]{:S(2)}, u32[]{:S(2)}) async-start(bf16[16,8,1000]{2,1,0:T(8,128)(2,1)} %broadcast_in_dim.17), calls=%async_computation | async-start | bytes 524288 | tf_op jit(solution)/shard_map/panel_points/all_to_all | solution.py:276
  17.8 0.7 pad_bitcast_fusion
  18.5 0.3 reduce-window.9
  18.9 0.1 slice_reduce_fusion
  19.1 0.7 fusion
  19.8 0.1 copy.10.starts
  19.9 0.1 copy.11.finish
  20.1 2.9 %copy.12.env = bf16[1024,1000]{1,0:T(8,128)(2,1)S(1)} copy(bf16[1024,1000]{0,1:T(8,128)(2,1)} %param.5) | data formatting | bytes 4096000 | tf_op args[0]
  23.0 2.2 all-to-all-done
  25.2 39.8 %all-gather = bf16[1,256,1000]{2,1,0:T(8,128)(2,1)S(1)} all-gather(bf16[1,8,1000]{2,1,0:T(8,128)(2,1)S(1)} %constant_dynamic-slice_fusion), channel_id=2, replica_groups=mesh['env'=32,'sp'=16] {'env'}, dimensions={1}, use_global_device_ids=true | all-gather | bytes 528000 | tf_op jit(solution)/shard_map/panel_points/all_gather | solution.py:278
  65.0 2.7 %panel.1 = (f32[512,256]{1,0:T(8,128)S(1)}, bf16[256,512]{1,0:T(8,128)(2,1)S(1)}, bf16[256,512]{1,0:T(8,128)(2,1)S(1)}, f32[256,256]{1,0:T(8,128)S(1)}, bf16[448,1024]{1,0:T(8,128)(2,1)S(1)}) custom-call(bf16[256,1000]{1,0:T(8,128)(2,1)S(1)} %bitcast.21, bf16[1024,1000]{1,0:T(8,128)(2,1)S(1)} %copy.12.env, bf16[64,1000]{1,0:T(8,128)(2,1)S(1)} %copy-done.2, ...), custom_call_target="tpu_custom_call" | custom-call | tf_op jit(solution)/shard_map/panel/pallas_call | solution.py:73
  67.7 0.9 copy-done.4
  68.7 0.8 copy.14
  69.5 7.0 %all-to-all-start.1 = ((f32[32,8,256]{2,1,0:T(8,128)}), f32[32,8,256]{2,1,0:T(8,128)S(1)}, u32[]{:S(2)}, u32[]{:S(2)}) async-start(f32[32,8,256]{2,1,0:T(8,128)} %bitcast.13), calls=%async_computation.1 | async-start | bytes 524288 | tf_op jit(solution)/shard_map/gram/all_to_all | solution.py:292
  76.6 0.8 copy.13.inverse
  77.4 0.6 pad_add_fusion.place.core
  78.0 14.4 %all-gather.3.cloned.1.call-done = bf16[5,256,1000]{2,1,0:T(8,128)(2,1)} async-done(((bf16[5,8,1000]{2,1,0:T(8,128)(2,1)}), bf16[5,256,1000]{2,1,0:T(8,128)(2,1)}) %all-gather.3.cloned.1.call-update) | async-done | bytes 2560016 | tf_op jit(solution)/shard_map/all_gather | solution.py:271
  92.4 12.7 %design.1 = (f32[512,1280]{1,0:T(8,128)}, f32[128,1280]{1,0:T(8,128)}, f32[128,1280]{1,0:T(8,128)}) custom-call(s32[2]{0:T(128)} %pad_add_fusion.place.core, bf16[1280,1000]{1,0:T(8,128)(2,1)} %bitcast.27, bf16[1024,1000]{1,0:T(8,128)(2,1)} %copy-done, bf16[64,1000]{1,0:T(8,128)(2,1)} %reg.3, bf16[448,1024]{1,0:T(8,128)(2,1)} %copy-done.4, ...), custom_call_target="tpu_custom_call" | custom-call | flops 7000000000 | bytes 9000000 | tf_op jit(solution)/shard_map/design/pallas_call | solution.py:109
  105.2 2.2 collective-permute-start
  107.4 2.0 collective-permute-done
  109.4 2.0 add_bitcast_fusion
  111.4 7.7 %all-to-all-start.2 = ((f32[16,8,1280]{2,1,0:T(8,128)}), f32[16,8,1280]{2,1,0:T(8,128)}, u32[]{:S(2)}, u32[]{:S(2)}) async-start(f32[16,8,1280]{2,1,0:T(8,128)} %add_bitcast_fusion), calls=%async_computation.2 | async-start | bytes 1310720 | tf_op jit(solution)/shard_map/product/all_to_all | solution.py:303
  119.1 29.0 %all-to-all-done.2 = f32[16,8,1280]{2,1,0:T(8,128)} async-done(((f32[16,8,1280]{2,1,0:T(8,128)}), f32[16,8,1280]{2,1,0:T(8,128)}, u32[]{:S(2)}, u32[]{:S(2)}) %all-to-all-start.2) | async-done | bytes 655392 | tf_op jit(solution)/shard_map/product/all_to_all | solution.py:303
  148.2 1.1 reduce_sum.18
  149.3 29.8 %all_gather.11.own = f32[128,1536]{1,0:T(8,128)S(1)} all-gather(f32[8,1536]{1,0:T(8,128)S(1)} %pad_maximum_fusion), channel_id=1, replica_groups={{0,32,64,96,128,160,192,224,256,288,320,352,384,416,448,480},{16,48,80,..., dimensions={0}, use_global_device_ids=true | all-gather | bytes 835584 | tf_op jit(solution)/shard_map/product/all_gather | solution.py:305
  179.1 13.3 %collective-permute-start.1 = (f32[128,1536]{1,0:T(8,128)S(1)}, f32[128,1536]{1,0:T(8,128)S(1)}, u32[]{:S(2)}, u32[]{:S(2)}) collective-permute-start(f32[128,1536]{1,0:T(8,128)S(1)} %all_gather.11.own), channel_id=1, source_target_pairs={{0,16},{16,0},{32,48},{48,32},{64,80},{80,64},{96,112},{112,96},{1... | collective-permute-start | bytes 2359304 | tf_op jit(solution)/shard_map/product/ppermute | solution.py:306
  192.4 1.7 collective-permute-done.1.other
  194.2 45.9 %factor.1.inverse_factor = f32[256,256]{1,0:T(8,128)S(1)} custom-call(s32[2]{0:T(128)S(1)} %copy-done.3, f32[128,1536]{1,0:T(8,128)S(1)} %all_gather.11.own, f32[128,1536]{1,0:T(8,128)S(1)} %collective-permute-done.1.other), custom_call_target="tpu_custom_call" | custom-call | tf_op jit(solution)/shard_map/factor/pallas_call | solution.py:194
  240.1 4.0 %update.1 = (f32[512,1280]{1,0:T(8,128)}, f32[256,1280]{1,0:T(8,128)}) custom-call(s32[2]{0:T(128)S(1)} %copy-done.3, f32[512,1280]{1,0:T(8,128)S(1)} %copy-done.1, f32[128,1536]{1,0:T(8,128)S(1)} %all_gather.11.own, f32[128,1536]{1,0:T(8,128)S(1)} %collective-permute-done.1.other, f32[256,256]{1,0:T(8,128)S(1)} %factor.1.inverse_factor, ...), custom_call_target="tpu_custom_call" | custom-call | tf_op jit(solution)/shard_map/update/pallas_call | solution.py:239
  (25 shorter events, 0.4 us)
Async XLA Ops:
  7.2 85.3 %all-gather.3.cloned.1.call-start = ((), (), s32[]{:S(2)}) async-start(), calls=%async_computation.3 | async-start | bytes 2703360 | tf_op jit(solution)/shard_map/all_gather | solution.py:271
  10.0 12.9 %copy-start.7 = (s32[1,448]{1,0:T(1,128)S(1)}, s32[1,448]{1,0:T(1,128)}, u32[]{:S(2)}) copy-start(s32[1,448]{1,0:T(1,128)} %param.6) | copy-start | bytes 5380
  10.0 15.1 %all-to-all-start = ((bf16[16,8,1000]{2,1,0:T(8,128)(2,1)}), bf16[16,8,1000]{2,1,0:T(8,128)(2,1)S(1)}, u32[]{:S(2)}, u32[]{:S(2)}) async-start(bf16[16,8,1000]{2,1,0:T(8,128)(2,1)} %broadcast_in_dim.17), calls=%async_computation | async-start | bytes 524288 | tf_op jit(solution)/shard_map/panel_points/all_to_all | solution.py:276
  17.8 47.2 %copy-start.2 = (bf16[64,1000]{1,0:T(8,128)(2,1)S(1)}, bf16[64,1000]{1,0:T(8,128)(2,1)}, u32[]{:S(2)}) copy-start(bf16[64,1000]{1,0:T(8,128)(2,1)} %reg.3) | copy-start | bytes 384004
  22.9 69.5 %copy-start = (bf16[1024,1000]{1,0:T(8,128)(2,1)}, bf16[1024,1000]{1,0:T(8,128)(2,1)S(1)}, u32[]{:S(2)}) copy-start(bf16[1024,1000]{1,0:T(8,128)(2,1)S(1)} %copy.12.env) | copy-start | bytes 6144004
  67.7 0.9 copy-start.4
  68.6 0.8 copy-start.5
  68.6 0.9 copy-start.6
  69.5 35.6 %all-to-all-start.1 = ((f32[32,8,256]{2,1,0:T(8,128)}), f32[32,8,256]{2,1,0:T(8,128)S(1)}, u32[]{:S(2)}, u32[]{:S(2)}) async-start(f32[32,8,256]{2,1,0:T(8,128)} %bitcast.13), calls=%async_computation.1 | async-start | bytes 524288 | tf_op jit(solution)/shard_map/gram/all_to_all | solution.py:292
  105.2 89.0 %copy-start.3 = (s32[2]{0:T(128)S(1)}, s32[2]{0:T(128)}, u32[]{:S(2)}) copy-start(s32[2]{0:T(128)} %pad_add_fusion.place.core) | copy-start | bytes 28
  105.2 4.2 %collective-permute-start = (f32[128,1280]{1,0:T(8,128)}, f32[128,1280]{1,0:T(8,128)S(1)}, u32[]{:S(2)}, u32[]{:S(2)}) collective-permute-start(f32[128,1280]{1,0:T(8,128)} %get-tuple-element.19), channel_id=1, source_target_pairs={{0,16},{16,0},{32,48},{48,32},{64,80},{80,64},{96,112},{112,96},{1... | collective-permute-start | bytes 1966088 | tf_op jit(solution)/shard_map/product/ppermute | solution.py:301
  111.4 128.7 %copy-start.1 = (f32[512,1280]{1,0:T(8,128)S(1)}, f32[512,1280]{1,0:T(8,128)}, u32[]{:S(2)}) copy-start(f32[512,1280]{1,0:T(8,128)} %get-tuple-element.15.design) | copy-start | bytes 7864324
  111.4 36.7 %all-to-all-start.2 = ((f32[16,8,1280]{2,1,0:T(8,128)}), f32[16,8,1280]{2,1,0:T(8,128)}, u32[]{:S(2)}, u32[]{:S(2)}) async-start(f32[16,8,1280]{2,1,0:T(8,128)} %add_bitcast_fusion), calls=%async_computation.2 | async-start | bytes 1310720 | tf_op jit(solution)/shard_map/product/all_to_all | solution.py:303
  179.1 15.0 %collective-permute-start.1 = (f32[128,1536]{1,0:T(8,128)S(1)}, f32[128,1536]{1,0:T(8,128)S(1)}, u32[]{:S(2)}, u32[]{:S(2)}) collective-permute-start(f32[128,1536]{1,0:T(8,128)S(1)} %all_gather.11.own), channel_id=1, source_target_pairs={{0,16},{16,0},{32,48},{48,32},{64,80},{80,64},{96,112},{112,96},{1... | collective-permute-start | bytes 2359304 | tf_op jit(solution)/shard_map/product/ppermute | solution.py:306
Sparse Core Ops, SparseCore 0:
  10.1 82.2 all-gather.2

commit v3 on v2

--- a/solution.py
+++ b/solution.py
@@ -18,6 +18,11 @@
 COLS = SLOTS * PANEL
 HALF = PANEL // 2
 START = 0.95
+LANES = 128
+TILES = COLS // LANES
+LOW = 3
+CODE = (TILES + LOW) * LANES
+FIXED = 524286.0
 
 cube_scale = 15.0 ** (-0.5)
 dot_scale = DESC ** (-0.5)
@@ -126,6 +131,63 @@
     )(place, *arrays)
 
 
+def tile_of(t):
+    return slice(t * LANES, (t + 1) * LANES)
+
+
+def code_kernel(keep, received, code_ref):
+    lane = lax.broadcasted_iota(jnp.int32, (HALF, LANES), 1)
+    low = [jnp.zeros((HALF, LANES), jnp.int32) for _ in range(LOW)]
+    for t in range(TILES):
+        x = keep[:, tile_of(t)] + received[:, tile_of(t)]
+        largest = jnp.maximum(jnp.max(jnp.abs(x), 1, keepdims=True), 1e-30)
+        exponent = jnp.minimum(jnp.ceil(jnp.log2(largest) + 1e-4), 127.0)
+        scaled = jnp.clip(x * (jnp.exp2(-exponent) * FIXED), -FIXED, FIXED)
+        rounded = jnp.where(scaled < 0, scaled - 0.5, scaled + 0.5).astype(jnp.int32)
+        code_ref[:, tile_of(t)] = (rounded >> 4).astype(jnp.int16)
+        low[t // 4] = low[t // 4] + ((rounded & 15) << (4 * (t % 4)))
+        low[-1] = low[-1] + jnp.where(lane == t, (exponent.astype(jnp.int32) + 128) << 8, 0)
+    for k in range(LOW):
+        code_ref[:, tile_of(TILES + k)] = (low[k] - 32768).astype(jnp.int16)
+
+
+def sum_kernel(code, pieces, rows_ref):
+    lane = lax.broadcasted_iota(jnp.int32, (HALF, LANES), 1)
+    low = [code[:, tile_of(TILES + k)].astype(jnp.int32) + 32768 for k in range(LOW)]
+    exponents = (low[-1] >> 8) - 128
+    for t in range(TILES):
+        exponent = jnp.sum(jnp.where(lane == t, exponents, 0).astype(jnp.float32), 1, keepdims=True)
+        fixed = code[:, tile_of(t)].astype(jnp.int32) * 16 + ((low[t // 4] >> (4 * (t % 4))) & 15)
+        x = fixed.astype(jnp.float32) * (jnp.exp2(exponent) * (1.0 / FIXED))
+        rows_ref[:, tile_of(t)] = jnp.sum(x.reshape(N_Z, HALF // N_Z, LANES), 0)
+    rows_ref[:, COLS:] = jnp.sum(pieces[...], 0)
+
+
+def code_step(keep, received):
+    half = pl.BlockSpec((HALF, COLS), lambda t: (0, 0))
+    return pl.pallas_call(
+        code_kernel,
+        grid=(1,),
+        in_specs=[half, half],
+        out_specs=pl.BlockSpec((HALF, CODE), lambda t: (0, 0)),
+        out_shape=jax.ShapeDtypeStruct((HALF, CODE), jnp.int16),
+        compiler_params=pltpu.CompilerParams(vmem_limit_bytes=DESIGN_VMEM),
+        name="code",
+    )(keep, received)
+
+
+def sum_step(code, pieces):
+    vmem = pl.BlockSpec(memory_space=pltpu.VMEM)
+    return pl.pallas_call(
+        sum_kernel,
+        in_specs=[vmem, vmem],
+        out_specs=vmem,
+        out_shape=jax.ShapeDtypeStruct((HALF // N_Z, COLS + PANEL), jnp.float32),
+        compiler_params=pltpu.CompilerParams(vmem_limit_bytes=VMEM_LIMIT),
+        name="sum",
+    )(code, pieces)
+
+
 FULL = dict(precision=lax.Precision.HIGHEST, preferred_element_type=jnp.float32)
 
 
@@ -298,10 +360,10 @@
 
     with jax.named_scope("product"):
         send, pieces = lax.optimization_barrier((send, pieces))
-        keep = keep + lax.ppermute(send, "env", CORE_SWAP)
-        keep = keep.reshape(N_Z, HALF // N_Z, COLS)
-        keep = lax.all_to_all(keep, "env", 0, 0, axis_index_groups=SAME_CORE)
-        rows = jnp.concatenate([jnp.sum(keep, 0), jnp.sum(pieces, 0)], 1)
+        code = code_step(keep, lax.ppermute(send, "env", CORE_SWAP))
+        code = code.reshape(N_Z, HALF // N_Z, CODE)
+        code = lax.all_to_all(code, "env", 0, 0, axis_index_groups=SAME_CORE)
+        rows = sum_step(code.reshape(HALF, CODE), pieces)
         own = lax.all_gather(rows, "env", axis=0, tiled=True, axis_index_groups=SAME_CORE)
         other = lax.ppermute(own, "env", CORE_SWAP)
 

time: 254 us -> 245 us (0.965)
  waiting for transfers between devices: 50 us -> 21.2 us
  blocking collectives: 69.6 us -> 97.9 us
  starting transfers between devices: 37.9 us -> 29.2 us
  other arithmetic: 4.92 us -> 1.71 us
  Pallas kernels: 65.4 us -> 68.5 us
    all_to_all x1 -> x0, waiting for transfers between devices: 29 us -> none  [shards(): keep = lax.all_to_all(keep, 'env', 0, 0, axis_index_groups=SAME_CORE)]
    all_to_all x0 -> x1, blocking collectives: none -> 27.6 us  [shards(): code = lax.all_to_all(code, 'env', 0, 0, axis_index_groups=SAME_CORE)]
    all_to_all x1 -> x0, starting transfers between devices: 7.66 us -> none  [shards(): keep = lax.all_to_all(keep, 'env', 0, 0, axis_index_groups=SAME_CORE)]
    pallas_call x0 -> x2, Pallas kernels: none -> 3.15 us  [the longest x1 2.88 us: code_step(): pl.pallas_call(code_kernel, grid=(1,), in_specs=[half, half], out_specs=p...]
  transfers between devices with their start and end apart: 6 -> 5, of which waited for: 5 -> 4; matrix products, arithmetic and copies ran while one was open for 4% -> 4% of each run, Pallas kernels for 6% -> 6%
where the time goes in v3:
time: 245 us; the launch traced here: 242 us
  blocking collectives  97.9 us (40%)
  Pallas kernels  68.5 us (28%)
  starting transfers between devices  29.2 us (12%)
  waiting for transfers between devices  21.2 us (9%)
  between operations  14.9 us (6%)
  local copies, waits for them, and re-layouts  8.99 us (4%)
    pallas_call x1, Pallas kernels, factor_step(): pl.pallas_call(factor_kernel, grid_spec=pltpu.PrefetchScalarGridSpec(num_...  45.9 us
    all_gather x1, blocking collectives, shards(): panel_points = lax.all_gather(mine, 'env', axis=0, tiled=True)  39.8 us
    all_gather x1, blocking collectives, shards(): lax.all_gather(rows, 'env', axis=0, tiled=True, axis_index_groups=SAME_CORE)  30.5 us
    all_to_all x1, blocking collectives, shards(): code = lax.all_to_all(code, 'env', 0, 0, axis_index_groups=SAME_CORE)  27.6 us
    all_gather x1, waiting for transfers between devices, shards(): gathered = lax.all_gather(sparse_desc, 'env', axis=1, tiled=True)  14.5 us
    pallas_call x1, Pallas kernels, design_step(): pl.pallas_call(design_kernel, grid_spec=pltpu.PrefetchScalarGridSpec(num_...  12.7 us
    ppermute x1, starting transfers between devices, shards(): other = lax.ppermute(own, 'env', CORE_SWAP)  12.3 us
    all_to_all x1, starting transfers between devices, shards(): offered = lax.all_to_all(offered, 'sp', 0, 0)  7.72 us
  transfers between devices with their start and end apart: 5, of which 4 were waited for; matrix products, arithmetic and copies ran while one was open for 4% of the time, Pallas kernels for 6%

profile of v3, /device:TPU:1, one launch (start us, length us, event | category | flops | bytes accessed | tf_op | source)
XLA Modules:
  0.0 242.5 jit_solution(7180889053032009699)
XLA Ops:
  7.2 0.7 all-gather.3.cloned.1.call-update
  8.6 0.7 dynamic-slice_bitcast_fusion
  9.3 0.7 broadcast_in_dim.17
  10.0 7.7 %all-to-all-start = ((bf16[16,8,1000]{2,1,0:T(8,128)(2,1)}), bf16[16,8,1000]{2,1,0:T(8,128)(2,1)S(1)}, u32[]{:S(2)}, u32[]{:S(2)}) async-start(bf16[16,8,1000]{2,1,0:T(8,128)(2,1)} %broadcast_in_dim.17), calls=%async_computation | async-start | bytes 524288 | tf_op jit(solution)/shard_map/panel_points/all_to_all | solution.py:338
  17.8 0.7 pad_bitcast_fusion
  18.5 0.3 reduce-window.9
  18.9 0.1 slice_reduce_fusion
  19.1 0.7 fusion
  19.8 0.1 copy.11.starts
  19.9 0.1 copy.12.finish
  20.1 2.9 %copy.13.env = bf16[1024,1000]{1,0:T(8,128)(2,1)S(1)} copy(bf16[1024,1000]{0,1:T(8,128)(2,1)} %param.5) | data formatting | bytes 4096000 | tf_op args[0]
  23.0 2.2 all-to-all-done
  25.2 39.8 %all-gather = bf16[1,256,1000]{2,1,0:T(8,128)(2,1)S(1)} all-gather(bf16[1,8,1000]{2,1,0:T(8,128)(2,1)S(1)} %constant_dynamic-slice_fusion), channel_id=2, replica_groups=mesh['env'=32,'sp'=16] {'env'}, dimensions={1}, use_global_device_ids=true | all-gather | bytes 528000 | tf_op jit(solution)/shard_map/panel_points/all_gather | solution.py:340
  65.0 2.7 %panel.1 = (f32[512,256]{1,0:T(8,128)S(1)}, bf16[256,512]{1,0:T(8,128)(2,1)S(1)}, bf16[256,512]{1,0:T(8,128)(2,1)S(1)}, f32[256,256]{1,0:T(8,128)S(1)}, bf16[448,1024]{1,0:T(8,128)(2,1)S(1)}) custom-call(bf16[256,1000]{1,0:T(8,128)(2,1)S(1)} %bitcast.21, bf16[1024,1000]{1,0:T(8,128)(2,1)S(1)} %copy.13.env, bf16[64,1000]{1,0:T(8,128)(2,1)S(1)} %copy-done.2, ...), custom_call_target="tpu_custom_call" | custom-call | tf_op jit(solution)/shard_map/panel/pallas_call | solution.py:78
  67.7 0.9 copy-done.4
  68.7 0.8 copy.15
  69.5 7.0 %all-to-all-start.1 = ((f32[32,8,256]{2,1,0:T(8,128)}), f32[32,8,256]{2,1,0:T(8,128)S(1)}, u32[]{:S(2)}, u32[]{:S(2)}) async-start(f32[32,8,256]{2,1,0:T(8,128)} %bitcast.13), calls=%async_computation.1 | async-start | bytes 524288 | tf_op jit(solution)/shard_map/gram/all_to_all | solution.py:354
  76.6 0.8 copy.14.inverse
  77.4 0.6 pad_add_fusion.place.core
  78.0 14.5 %all-gather.3.cloned.1.call-done = bf16[5,256,1000]{2,1,0:T(8,128)(2,1)} async-done(((bf16[5,8,1000]{2,1,0:T(8,128)(2,1)}), bf16[5,256,1000]{2,1,0:T(8,128)(2,1)}) %all-gather.3.cloned.1.call-update) | async-done | bytes 2560016 | tf_op jit(solution)/shard_map/all_gather | solution.py:333
  92.4 12.7 %design.1 = (f32[512,1280]{1,0:T(8,128)}, f32[128,1280]{1,0:T(8,128)}, f32[128,1280]{1,0:T(8,128)}) custom-call(s32[2]{0:T(128)} %pad_add_fusion.place.core, bf16[1280,1000]{1,0:T(8,128)(2,1)} %bitcast.29, bf16[1024,1000]{1,0:T(8,128)(2,1)} %copy-done, bf16[64,1000]{1,0:T(8,128)(2,1)} %reg.3, bf16[448,1024]{1,0:T(8,128)(2,1)} %copy-done.4, ...), custom_call_target="tpu_custom_call" | custom-call | flops 7000000000 | bytes 9000000 | tf_op jit(solution)/shard_map/design/pallas_call | solution.py:114
  105.2 2.2 collective-permute-start
  107.4 2.0 collective-permute-done.received
  109.4 0.8 copy-done.7
  110.2 2.9 %code.1 = s16[128,1664]{1,0:T(8,128)(2,1)} custom-call(f32[128,1280]{1,0:T(8,128)} %get-tuple-element.16.keep, f32[128,1280]{1,0:T(8,128)} %copy-done.7), custom_call_target="tpu_custom_call" | custom-call | tf_op jit(solution)/shard_map/product/code/pallas_call | solution.py:168
  113.1 27.6 %all_to_all.15 = s16[16,8,1664]{2,1,0:T(8,128)(2,1)S(1)} all-to-all(s16[16,8,1664]{2,1,0:T(8,128)(2,1)} %bitcast.24), channel_id=1, replica_groups={{0,32,64,96,128,160,192,224,256,288,320,352,384,416,448,480},{16,48,80,..., dimensions={0} | all-to-all | bytes 851968 | tf_op jit(solution)/shard_map/product/all_to_all | solution.py:365
  140.7 0.3 sum.1
  141.0 30.5 %all_gather.11.own = f32[128,1536]{1,0:T(8,128)S(1)} all-gather(f32[8,1536]{1,0:T(8,128)S(1)} %sum.1), channel_id=1, replica_groups={{0,32,64,96,128,160,192,224,256,288,320,352,384,416,448,480},{16,48,80,..., dimensions={0}, use_global_device_ids=true | all-gather | bytes 835584 | tf_op jit(solution)/shard_map/product/all_gather | solution.py:367
  171.5 12.3 %collective-permute-start.1 = (f32[128,1536]{1,0:T(8,128)S(1)}, f32[128,1536]{1,0:T(8,128)S(1)}, u32[]{:S(2)}, u32[]{:S(2)}) collective-permute-start(f32[128,1536]{1,0:T(8,128)S(1)} %all_gather.11.own), channel_id=1, source_target_pairs={{0,16},{16,0},{32,48},{48,32},{64,80},{80,64},{96,112},{112,96},{1... | collective-permute-start | bytes 2359304 | tf_op jit(solution)/shard_map/product/ppermute | solution.py:368
  183.8 1.9 collective-permute-done.1.other
  185.7 45.9 %factor.1.inverse_factor = f32[256,256]{1,0:T(8,128)S(1)} custom-call(s32[2]{0:T(128)S(1)} %copy-done.3, f32[128,1536]{1,0:T(8,128)S(1)} %all_gather.11.own, f32[128,1536]{1,0:T(8,128)S(1)} %collective-permute-done.1.other), custom_call_target="tpu_custom_call" | custom-call | tf_op jit(solution)/shard_map/factor/pallas_call | solution.py:256
  231.6 4.0 %update.1 = (f32[512,1280]{1,0:T(8,128)}, f32[256,1280]{1,0:T(8,128)}) custom-call(s32[2]{0:T(128)S(1)} %copy-done.3, f32[512,1280]{1,0:T(8,128)S(1)} %copy-done.1, f32[128,1536]{1,0:T(8,128)S(1)} %all_gather.11.own, f32[128,1536]{1,0:T(8,128)S(1)} %collective-permute-done.1.other, f32[256,256]{1,0:T(8,128)S(1)} %factor.1.inverse_factor, ...), custom_call_target="tpu_custom_call" | custom-call | tf_op jit(solution)/shard_map/update/pallas_call | solution.py:301
  (24 shorter events, 0.4 us)
Async XLA Ops:
  7.2 85.3 %all-gather.3.cloned.1.call-start = ((), (), s32[]{:S(2)}) async-start(), calls=%async_computation.3 | async-start | bytes 2703360 | tf_op jit(solution)/shard_map/all_gather | solution.py:333
  10.0 12.9 %copy-start.8 = (s32[1,448]{1,0:T(1,128)S(1)}, s32[1,448]{1,0:T(1,128)}, u32[]{:S(2)}) copy-start(s32[1,448]{1,0:T(1,128)} %param.6) | copy-start | bytes 5380
  10.0 15.1 %all-to-all-start = ((bf16[16,8,1000]{2,1,0:T(8,128)(2,1)}), bf16[16,8,1000]{2,1,0:T(8,128)(2,1)S(1)}, u32[]{:S(2)}, u32[]{:S(2)}) async-start(bf16[16,8,1000]{2,1,0:T(8,128)(2,1)} %broadcast_in_dim.17), calls=%async_computation | async-start | bytes 524288 | tf_op jit(solution)/shard_map/panel_points/all_to_all | solution.py:338
  17.8 47.2 %copy-start.2 = (bf16[64,1000]{1,0:T(8,128)(2,1)S(1)}, bf16[64,1000]{1,0:T(8,128)(2,1)}, u32[]{:S(2)}) copy-start(bf16[64,1000]{1,0:T(8,128)(2,1)} %reg.3) | copy-start | bytes 384004
  22.9 69.5 %copy-start = (bf16[1024,1000]{1,0:T(8,128)(2,1)}, bf16[1024,1000]{1,0:T(8,128)(2,1)S(1)}, u32[]{:S(2)}) copy-start(bf16[1024,1000]{1,0:T(8,128)(2,1)S(1)} %copy.13.env) | copy-start | bytes 6144004
  67.7 0.9 copy-start.4
  68.6 0.8 copy-start.5
  68.6 0.9 copy-start.6
  69.5 35.6 %all-to-all-start.1 = ((f32[32,8,256]{2,1,0:T(8,128)}), f32[32,8,256]{2,1,0:T(8,128)S(1)}, u32[]{:S(2)}, u32[]{:S(2)}) async-start(f32[32,8,256]{2,1,0:T(8,128)} %bitcast.13), calls=%async_computation.1 | async-start | bytes 524288 | tf_op jit(solution)/shard_map/gram/all_to_all | solution.py:354
  105.2 80.5 %copy-start.3 = (s32[2]{0:T(128)S(1)}, s32[2]{0:T(128)}, u32[]{:S(2)}) copy-start(s32[2]{0:T(128)} %pad_add_fusion.place.core) | copy-start | bytes 28
  105.2 4.2 %collective-permute-start = (f32[128,1280]{1,0:T(8,128)}, f32[128,1280]{1,0:T(8,128)S(1)}, u32[]{:S(2)}, u32[]{:S(2)}) collective-permute-start(f32[128,1280]{1,0:T(8,128)} %get-tuple-element.19), channel_id=1, source_target_pairs={{0,16},{16,0},{32,48},{48,32},{64,80},{80,64},{96,112},{112,96},{1... | collective-permute-start | bytes 1966088 | tf_op jit(solution)/shard_map/product/ppermute | solution.py:363
  109.4 0.8 copy-start.7
  110.2 121.4 %copy-start.1 = (f32[512,1280]{1,0:T(8,128)S(1)}, f32[512,1280]{1,0:T(8,128)}, u32[]{:S(2)}) copy-start(f32[512,1280]{1,0:T(8,128)} %get-tuple-element.15.design) | copy-start | bytes 7864324
  171.5 14.2 %collective-permute-start.1 = (f32[128,1536]{1,0:T(8,128)S(1)}, f32[128,1536]{1,0:T(8,128)S(1)}, u32[]{:S(2)}, u32[]{:S(2)}) collective-permute-start(f32[128,1536]{1,0:T(8,128)S(1)} %all_gather.11.own), channel_id=1, source_target_pairs={{0,16},{16,0},{32,48},{48,32},{64,80},{80,64},{96,112},{112,96},{1... | collective-permute-start | bytes 2359304 | tf_op jit(solution)/shard_map/product/ppermute | solution.py:368
Sparse Core Ops, SparseCore 0:
  10.1 82.2 all-gather.2

commit v4 on v3

--- a/solution.py
+++ b/solution.py
@@ -23,6 +23,9 @@
 LOW = 3
 CODE = (TILES + LOW) * LANES
 FIXED = 524286.0
+GRAM_FIXED = 8388606.0
+WIDE = CODE + 3 * LANES
+GRAM_LOW = TILES + LOW
 
 cube_scale = 15.0 ** (-0.5)
 dot_scale = DESC ** (-0.5)
@@ -102,9 +105,10 @@
     hi, lo = halves(rows_ref[...])
     left = panel_hi[...]
     product = nn(left, hi) + nn(left, lo) + nn(panel_lo[...], hi)
+    product = product.reshape(N_Z, 2, HALF // N_Z, COLS)
     first = place[0] == 0
-    keep_ref[...] = jnp.where(first, product[:HALF], product[HALF:])
-    send_ref[...] = jnp.where(first, product[HALF:], product[:HALF])
+    keep_ref[...] = jnp.where(first, product[:, 0], product[:, 1]).reshape(HALF, COLS)
+    send_ref[...] = jnp.where(first, product[:, 1], product[:, 0]).reshape(HALF, COLS)
     leave.wait()
 
 
@@ -135,32 +139,64 @@
     return slice(t * LANES, (t + 1) * LANES)
 
 
-def code_kernel(keep, received, code_ref):
-    lane = lax.broadcasted_iota(jnp.int32, (HALF, LANES), 1)
-    low = [jnp.zeros((HALF, LANES), jnp.int32) for _ in range(LOW)]
-    for t in range(TILES):
-        x = keep[:, tile_of(t)] + received[:, tile_of(t)]
-        largest = jnp.maximum(jnp.max(jnp.abs(x), 1, keepdims=True), 1e-30)
-        exponent = jnp.minimum(jnp.ceil(jnp.log2(largest) + 1e-4), 127.0)
-        scaled = jnp.clip(x * (jnp.exp2(-exponent) * FIXED), -FIXED, FIXED)
-        rounded = jnp.where(scaled < 0, scaled - 0.5, scaled + 0.5).astype(jnp.int32)
+def fixed_point(x, limit):
+    largest = jnp.maximum(jnp.max(jnp.abs(x), 1, keepdims=True), 1e-30)
+    exponent = jnp.minimum(jnp.ceil(jnp.log2(largest) + 1e-4), 127.0)
+    scaled = jnp.clip(x * (jnp.exp2(-exponent) * limit), -limit, limit)
+    return jnp.where(scaled < 0, scaled - 0.5, scaled + 0.5).astype(jnp.int32), exponent.astype(jnp.int32) + 128
+
+
+def encode(tiles, code_ref):
+    rows = code_ref.shape[0]
+    lane = lax.broadcasted_iota(jnp.int32, (rows, LANES), 1)
+    low = [jnp.zeros((rows, LANES), jnp.int32) for _ in range(LOW)]
+    for t, x in enumerate(tiles):
+        rounded, exponent = fixed_point(x, FIXED)
         code_ref[:, tile_of(t)] = (rounded >> 4).astype(jnp.int16)
         low[t // 4] = low[t // 4] + ((rounded & 15) << (4 * (t % 4)))
-        low[-1] = low[-1] + jnp.where(lane == t, (exponent.astype(jnp.int32) + 128) << 8, 0)
+        low[-1] = low[-1] + jnp.where(lane == t, exponent << 8, 0)
+    return low, lane
+
+
+def unsigned(code):
+    return code.astype(jnp.int32) + 32768
+
+
+def unit(exponents, t, limit):
+    lane = lax.broadcasted_iota(jnp.int32, exponents.shape, 1)
+    exponent = jnp.sum(jnp.where(lane == t, (exponents >> 8) - 128, 0).astype(jnp.float32), 1, keepdims=True)
+    return jnp.exp2(exponent) * (1.0 / limit)
+
+
+def decode(high, low, shift, exponents, t):
+    number = high.astype(jnp.int32) * 16 + ((low >> shift) & 15)
+    return number.astype(jnp.float32) * unit(exponents, t, FIXED)
+
+
+def code_kernel(keep, received, code_ref):
+    low, _ = encode([keep[:, tile_of(t)] + received[:, tile_of(t)] for t in range(TILES)], code_ref)
     for k in range(LOW):
         code_ref[:, tile_of(TILES + k)] = (low[k] - 32768).astype(jnp.int16)
 
 
-def sum_kernel(code, pieces, rows_ref):
-    lane = lax.broadcasted_iota(jnp.int32, (HALF, LANES), 1)
-    low = [code[:, tile_of(TILES + k)].astype(jnp.int32) + 32768 for k in range(LOW)]
-    exponents = (low[-1] >> 8) - 128
-    for t in range(TILES):
-        exponent = jnp.sum(jnp.where(lane == t, exponents, 0).astype(jnp.float32), 1, keepdims=True)
-        fixed = code[:, tile_of(t)].astype(jnp.int32) * 16 + ((low[t // 4] >> (4 * (t % 4))) & 15)
-        x = fixed.astype(jnp.float32) * (jnp.exp2(exponent) * (1.0 / FIXED))
-        rows_ref[:, tile_of(t)] = jnp.sum(x.reshape(N_Z, HALF // N_Z, LANES), 0)
-    rows_ref[:, COLS:] = jnp.sum(pieces[...], 0)
+def sum_kernel(code, pieces, code_ref):
+    low = [unsigned(code[:, tile_of(TILES + k)]) for k in range(LOW)]
+
+    def total(t):
+        x = decode(code[:, tile_of(t)], low[t // 4], 4 * (t % 4), low[-1], t)
+        return jnp.sum(x.reshape(N_Z, HALF // N_Z, LANES), 0)
+
+    out, lane = encode([total(t) for t in range(TILES)], code_ref)
+    gram = jnp.sum(pieces[...], 0)
+    gram_low = jnp.zeros((HALF // N_Z, LANES), jnp.int32)
+    for g in range(2):
+        rounded, exponent = fixed_point(gram[:, tile_of(g)], GRAM_FIXED)
+        code_ref[:, tile_of(TILES + LOW + 1 + g)] = (rounded >> 8).astype(jnp.int16)
+        gram_low = gram_low + ((rounded & 255) << (8 * g))
+        out[-1] = out[-1] + jnp.where(lane == TILES + g, exponent << 8, 0)
+    for k in range(LOW):
+        code_ref[:, tile_of(TILES + k)] = (out[k] - 32768).astype(jnp.int16)
+    code_ref[:, tile_of(GRAM_LOW)] = (gram_low - 32768).astype(jnp.int16)
 
 
 def code_step(keep, received):
@@ -182,7 +218,7 @@
         sum_kernel,
         in_specs=[vmem, vmem],
         out_specs=vmem,
-        out_shape=jax.ShapeDtypeStruct((HALF // N_Z, COLS + PANEL), jnp.float32),
+        out_shape=jax.ShapeDtypeStruct((HALF // N_Z, WIDE), jnp.int16),
         compiler_params=pltpu.CompilerParams(vmem_limit_bytes=VMEM_LIMIT),
         name="sum",
     )(code, pieces)
@@ -191,16 +227,20 @@
 FULL = dict(precision=lax.Precision.HIGHEST, preferred_element_type=jnp.float32)
 
 
-def stacked(core, own, other):
-    return jnp.where(core == 0, jnp.concatenate([own, other], 0), jnp.concatenate([other, own], 0))
-
-
-def factor_kernel(core, own, other, inv_ref, x_ref, s_ref):
+def factor_kernel(high, low, exponents, inv_ref, x_ref, s_ref):
     row = lax.broadcasted_iota(jnp.int32, (PANEL, PANEL), 0)
     col = lax.broadcasted_iota(jnp.int32, (PANEL, PANEL), 1)
     diag = (row == col).astype(jnp.float32)
     phi = jnp.where(row > col, 1.0, 0.5 * diag)
-    g = stacked(core[0], own[...], other[...])
+    low_bits = unsigned(low[...])
+    exps = unsigned(exponents[...])
+
+    def gram_tile(k):
+        number = high[:, tile_of(k)].astype(jnp.int32) * 256 + ((low_bits >> (8 * k)) & 255)
+        return number.astype(jnp.float32) * unit(exps, TILES + k, GRAM_FIXED)
+
+    g = jnp.concatenate([gram_tile(0), gram_tile(1)], 1)
+    g = jnp.where(row >= col, g, g.T)
     on_diag = g * diag
     d_row = lax.rsqrt(jnp.sum(on_diag, 0, keepdims=True))
     d_col = lax.rsqrt(jnp.sum(on_diag, 1, keepdims=True))
@@ -251,24 +291,27 @@
         inv_ref[...] = x_ref[...] * d_row
 
 
-def factor_step(place, own, other):
-    columns = pl.BlockSpec((HALF, PANEL), lambda t, s: (0, SLOTS))
+def factor_step(code):
+    tile = lambda k: pl.BlockSpec((PANEL, LANES), lambda t: (0, k))
     return pl.pallas_call(
         factor_kernel,
-        grid_spec=pltpu.PrefetchScalarGridSpec(
-            num_scalar_prefetch=1,
-            grid=(1,),
-            in_specs=[columns, columns],
-            out_specs=pl.BlockSpec((PANEL, PANEL), lambda t, s: (0, 0)),
-            scratch_shapes=[pltpu.VMEM((PANEL, PANEL), jnp.float32)] * 2,
-        ),
+        grid=(1,),
+        in_specs=[
+            pl.BlockSpec((PANEL, PANEL), lambda t: (0, (TILES + LOW + 1) // 2)),
+            tile(GRAM_LOW),
+            tile(TILES + LOW - 1),
+        ],
+        out_specs=pl.BlockSpec((PANEL, PANEL), lambda t: (0, 0)),
         out_shape=jax.ShapeDtypeStruct((PANEL, PANEL), jnp.float32),
+        scratch_shapes=[pltpu.VMEM((PANEL, PANEL), jnp.float32)] * 2,
         compiler_params=pltpu.CompilerParams(vmem_limit_bytes=VMEM_LIMIT),
         name="factor",
-    )(place, own, other)
-
-
-def update_kernel(place, design, own, other, inverse_factor, panel, updated_ref, coupling_ref, q_ref):
+    )(code, code, code)
+
+
+def update_kernel(
+    place, design, high, low, exponents, inverse_factor, panel, updated_ref, coupling_ref, q_ref
+):
     t = pl.program_id(0)
 
     @pl.when(t == 0)
@@ -285,7 +328,11 @@
     @pl.when(t >= place[1])
     def _():
         f_hi, f_lo = halves(inverse_factor[...])
-        w_hi, w_lo = halves(stacked(place[0], own[...], other[...]))
+        low_bits = unsigned(low[...]) >> (8 * lax.rem(t, 2))
+        exps = unsigned(exponents[...])
+        left = decode(high[:, tile_of(0)], low_bits, 0, exps, 2 * t)
+        right = decode(high[:, tile_of(1)], low_bits, 4, exps, 2 * t + 1)
+        w_hi, w_lo = halves(jnp.concatenate([left, right], 1))
         coupling = nn(f_hi, w_hi) + nn(f_hi, w_lo) + nn(f_lo, w_hi)
         coupling_ref[...] = coupling
         q_hi, q_lo = halves(q_ref[...])
@@ -297,7 +344,7 @@
         updated_ref[...] = q_ref[...]
 
 
-def update_step(place, design, own, other, inverse_factor, panel):
+def update_step(place, design, code, inverse_factor, panel):
     return pl.pallas_call(
         update_kernel,
         grid_spec=pltpu.PrefetchScalarGridSpec(
@@ -305,8 +352,9 @@
             grid=(SLOTS,),
             in_specs=[
                 pl.BlockSpec((ROWS, TILE), lambda t, s: (0, t)),
-                pl.BlockSpec((HALF, TILE), lambda t, s: (0, t)),
-                pl.BlockSpec((HALF, TILE), lambda t, s: (0, t)),
+                pl.BlockSpec((PANEL, TILE), lambda t, s: (0, t)),
+                pl.BlockSpec((PANEL, LANES), lambda t, s: (0, TILES + t // 2)),
+                pl.BlockSpec((PANEL, LANES), lambda t, s: (0, TILES + LOW - 1)),
                 pl.BlockSpec((PANEL, PANEL), lambda t, s: (0, 0)),
                 pl.BlockSpec((ROWS, PANEL), lambda t, s: (0, 0)),
             ],
@@ -322,7 +370,7 @@
         ),
         compiler_params=pltpu.CompilerParams(vmem_limit_bytes=VMEM_LIMIT),
         name="update",
-    )(place, design, own, other, inverse_factor, panel)
+    )(place, design, code, code, code, inverse_factor, panel)
 
 
 def shards(env_desc, env_counts, reg_desc, sparse_desc, panel_block):
@@ -349,8 +397,7 @@
     )
 
     with jax.named_scope("gram"):
-        pieces = gram.reshape(2, N_Z, HALF // N_Z, PANEL).swapaxes(0, 1)
-        pieces = pieces.reshape(2 * N_Z, HALF // N_Z, PANEL)
+        pieces = gram.reshape(2 * N_Z, HALF // N_Z, PANEL)
         pieces = lax.all_to_all(pieces, "env", 0, 0)
 
     points = gathered.reshape(COLS, DESC)
@@ -363,12 +410,10 @@
         code = code_step(keep, lax.ppermute(send, "env", CORE_SWAP))
         code = code.reshape(N_Z, HALF // N_Z, CODE)
         code = lax.all_to_all(code, "env", 0, 0, axis_index_groups=SAME_CORE)
-        rows = sum_step(code.reshape(HALF, CODE), pieces)
-        own = lax.all_gather(rows, "env", axis=0, tiled=True, axis_index_groups=SAME_CORE)
-        other = lax.ppermute(own, "env", CORE_SWAP)
-
-    inverse_factor = factor_step(place, own, other)
-    return update_step(place, design, own, other, inverse_factor, panel)
+        code = sum_step(code.reshape(HALF, CODE), pieces)
+        code = lax.all_gather(code, "env", axis=0, tiled=True)
+
+    return update_step(place, design, code, factor_step(code), panel)
 
 
 def solution(mesh):

time: 245 us -> 239 us (0.976)
  starting transfers between devices: 29.2 us -> 16.9 us
  blocking collectives: 97.9 us -> 106 us
  waiting for transfers between devices: 21.2 us -> 17.6 us
    ppermute x1 -> x0, starting transfers between devices: 12.3 us -> none  [shards(): other = lax.ppermute(own, 'env', CORE_SWAP)]
    all_gather x1, blocking collectives: 30.5 us -> 40 us  [shards(): code = lax.all_gather(code, 'env', axis=0, tiled=True)]
  transfers between devices with their start and end apart: 5 -> 4, of which waited for: 4 -> 3; matrix products, arithmetic and copies ran while one was open for 4% -> 3% of each run, Pallas kernels for 6% -> 7%
where the time goes in v4:
time: 239 us; the launch traced here: 237 us
  blocking collectives  106 us (44%)
  Pallas kernels  70.7 us (30%)
  waiting for transfers between devices  17.6 us (7%)
  starting transfers between devices  16.9 us (7%)
  between operations  14.9 us (6%)
  local copies, waits for them, and re-layouts  9.51 us (4%)
    pallas_call x1, Pallas kernels, factor_step(): pl.pallas_call(factor_kernel, grid=(1,), in_specs=[pl.BlockSpec((PANEL, P...  45.4 us
    all_gather x1, blocking collectives, shards(): code = lax.all_gather(code, 'env', axis=0, tiled=True)  40 us
    all_gather x1, blocking collectives, shards(): panel_points = lax.all_gather(mine, 'env', axis=0, tiled=True)  39.8 us
    all_to_all x1, blocking collectives, shards(): code = lax.all_to_all(code, 'env', 0, 0, axis_index_groups=SAME_CORE)  26.1 us
    all_gather x1, waiting for transfers between devices, shards(): gathered = lax.all_gather(sparse_desc, 'env', axis=1, tiled=True)  12.8 us
    pallas_call x1, Pallas kernels, design_step(): pl.pallas_call(design_kernel, grid_spec=pltpu.PrefetchScalarGridSpec(num_...  12.7 us
    all_to_all x1, starting transfers between devices, shards(): offered = lax.all_to_all(offered, 'sp', 0, 0)  7.72 us
    all_to_all x1, starting transfers between devices, shards(): pieces = lax.all_to_all(pieces, 'env', 0, 0)  6.99 us
  transfers between devices with their start and end apart: 4, of which 3 were waited for; matrix products, arithmetic and copies ran while one was open for 3% of the time, Pallas kernels for 7%

profile of v4, /device:TPU:1, one launch (start us, length us, event | category | flops | bytes accessed | tf_op | source)
XLA Modules:
  0.0 237.4 jit_solution(10940131762986856714)
XLA Ops:
  7.2 0.7 all-gather.4.cloned.1.call-update
  8.6 0.7 dynamic-slice_bitcast_fusion
  9.3 0.7 broadcast_in_dim.17
  10.0 7.7 %all-to-all-start = ((bf16[16,8,1000]{2,1,0:T(8,128)(2,1)}), bf16[16,8,1000]{2,1,0:T(8,128)(2,1)S(1)}, u32[]{:S(2)}, u32[]{:S(2)}) async-start(bf16[16,8,1000]{2,1,0:T(8,128)(2,1)} %broadcast_in_dim.17), calls=%async_computation | async-start | bytes 524288 | tf_op jit(solution)/shard_map/panel_points/all_to_all | solution.py:386
  17.8 0.7 pad_bitcast_fusion
  18.5 0.3 reduce-window.9
  18.8 0.1 slice.10
  18.9 0.1 slice_reduce_fusion
  19.1 0.7 fusion
  19.8 0.1 copy.10.starts
  19.9 0.1 copy.11.finish
  20.1 2.9 %copy.12.env = bf16[1024,1000]{1,0:T(8,128)(2,1)S(1)} copy(bf16[1024,1000]{0,1:T(8,128)(2,1)} %param.5) | data formatting | bytes 4096000 | tf_op args[0]
  23.0 2.2 all-to-all-done
  25.2 39.8 %all-gather = bf16[1,256,1000]{2,1,0:T(8,128)(2,1)S(1)} all-gather(bf16[1,8,1000]{2,1,0:T(8,128)(2,1)S(1)} %constant_dynamic-slice_fusion), channel_id=2, replica_groups=mesh['env'=32,'sp'=16] {'env'}, dimensions={1}, use_global_device_ids=true | all-gather | bytes 528000 | tf_op jit(solution)/shard_map/panel_points/all_gather | solution.py:388
  65.0 3.4 %panel.1 = (f32[512,256]{1,0:T(8,128)S(1)}, bf16[256,512]{1,0:T(8,128)(2,1)S(1)}, bf16[256,512]{1,0:T(8,128)(2,1)S(1)}, f32[256,256]{1,0:T(8,128)}, bf16[448,1024]{1,0:T(8,128)(2,1)S(1)}) custom-call(bf16[256,1000]{1,0:T(8,128)(2,1)S(1)} %bitcast.18, bf16[1024,1000]{1,0:T(8,128)(2,1)S(1)} %copy.12.env, bf16[64,1000]{1,0:T(8,128)(2,1)S(1)} %copy-done.2, ...), custom_call_target="tpu_custom_call" | custom-call | tf_op jit(solution)/shard_map/panel/pallas_call | solution.py:81
  68.4 0.9 copy-done.4
  69.3 0.7 copy-done.5
  70.0 0.7 copy-done.6
  70.7 7.0 %all-to-all-start.1 = ((f32[32,8,256]{2,1,0:T(8,128)}), f32[32,8,256]{2,1,0:T(8,128)S(1)}, u32[]{:S(2)}, u32[]{:S(2)}) async-start(f32[32,8,256]{2,1,0:T(8,128)} %bitcast.11), calls=%async_computation.1 | async-start | bytes 524288 | tf_op jit(solution)/shard_map/gram/all_to_all | solution.py:401
  77.8 0.8 copy.13.inverse
  78.6 0.6 pad_add_fusion.place
  79.2 12.8 %all-gather.4.cloned.1.call-done = bf16[5,256,1000]{2,1,0:T(8,128)(2,1)} async-done(((bf16[5,8,1000]{2,1,0:T(8,128)(2,1)}), bf16[5,256,1000]{2,1,0:T(8,128)(2,1)}) %all-gather.4.cloned.1.call-update) | async-done | bytes 2560016 | tf_op jit(solution)/shard_map/all_gather | solution.py:381
  92.0 12.7 %design.1 = (f32[512,1280]{1,0:T(8,128)}, f32[128,1280]{1,0:T(8,128)}, f32[128,1280]{1,0:T(8,128)}) custom-call(s32[2]{0:T(128)} %pad_add_fusion.place, bf16[1280,1000]{1,0:T(8,128)(2,1)} %bitcast.25, bf16[1024,1000]{1,0:T(8,128)(2,1)} %copy-done, bf16[64,1000]{1,0:T(8,128)(2,1)} %reg.3, bf16[448,1024]{1,0:T(8,128)(2,1)} %copy-done.4, ...), custom_call_target="tpu_custom_call" | custom-call | flops 7000000000 | bytes 9000000 | tf_op jit(solution)/shard_map/design/pallas_call | solution.py:118
  104.7 2.2 collective-permute-start
  106.9 2.0 collective-permute-done.received
  108.9 0.8 copy-done.7
  109.8 2.7 %code.1 = s16[128,1664]{1,0:T(8,128)(2,1)} custom-call(f32[128,1280]{1,0:T(8,128)} %get-tuple-element.16.keep, f32[128,1280]{1,0:T(8,128)} %copy-done.7), custom_call_target="tpu_custom_call" | custom-call | tf_op jit(solution)/shard_map/product/code/pallas_call | solution.py:204
  112.5 26.1 %all_to_all.15 = s16[16,8,1664]{2,1,0:T(8,128)(2,1)S(1)} all-to-all(s16[16,8,1664]{2,1,0:T(8,128)(2,1)} %bitcast.20), channel_id=1, replica_groups={{0,32,64,96,128,160,192,224,256,288,320,352,384,416,448,480},{16,48,80,..., dimensions={0} | all-to-all | bytes 851968 | tf_op jit(solution)/shard_map/product/all_to_all | solution.py:412
  138.6 0.4 sum.1
  139.0 40.0 %all-gather.5.high.low.exponents = s16[256,2048]{1,0:T(8,128)(2,1)S(1)} all-gather(s16[8,2048]{1,0:T(8,128)(2,1)S(1)} %sum.1), channel_id=1, replica_groups=mesh['env'=32,'sp'=16] {'env'}, dimensions={0}, use_global_device_ids=true | all-gather | bytes 1081344 | tf_op jit(solution)/shard_map/product/all_gather | solution.py:414
  179.0 45.4 %factor.1.inverse_factor = f32[256,256]{1,0:T(8,128)S(1)} custom-call(s16[256,2048]{1,0:T(8,128)(2,1)S(1)} %all-gather.5.high.low.exponents, s16[256,2048]{1,0:T(8,128)(2,1)S(1)} %all-gather.5.high.low.exponents, s16[256,2048]{1,0:T(8,128)(2,1)S(1)} %all-gather.5.high.low.exponents), custom_call_target="tpu_custom_call" | custom-call | tf_op jit(solution)/shard_map/factor/pallas_call | solution.py:296
  224.4 6.1 %update.1 = (f32[512,1280]{1,0:T(8,128)}, f32[256,1280]{1,0:T(8,128)}) custom-call(s32[2]{0:T(128)S(1)} %copy-done.3, f32[512,1280]{1,0:T(8,128)S(1)} %copy-done.1, s16[256,2048]{1,0:T(8,128)(2,1)S(1)} %all-gather.5.high.low.exponents, s16[256,2048]{1,0:T(8,128)(2,1)S(1)} %all-gather.5.high.low.exponents, s16[256,2048]{1,0:T(8,128)(2,1)S(1)} %all-gather.5.high.low.exponents, ...), custom_call_target="tpu_custom_call" | custom-call | tf_op jit(solution)/shard_map/update/pallas_call | solution.py:348
  (21 shorter events, 0.2 us)
Async XLA Ops:
  7.2 84.8 %all-gather.4.cloned.1.call-start = ((), (), s32[]{:S(2)}) async-start(), calls=%async_computation.3 | async-start | bytes 2703360 | tf_op jit(solution)/shard_map/all_gather | solution.py:381
  10.0 12.9 %copy-start.8 = (s32[1,448]{1,0:T(1,128)S(1)}, s32[1,448]{1,0:T(1,128)}, u32[]{:S(2)}) copy-start(s32[1,448]{1,0:T(1,128)} %param.6) | copy-start | bytes 5380
  10.0 15.1 %all-to-all-start = ((bf16[16,8,1000]{2,1,0:T(8,128)(2,1)}), bf16[16,8,1000]{2,1,0:T(8,128)(2,1)S(1)}, u32[]{:S(2)}, u32[]{:S(2)}) async-start(bf16[16,8,1000]{2,1,0:T(8,128)(2,1)} %broadcast_in_dim.17), calls=%async_computation | async-start | bytes 524288 | tf_op jit(solution)/shard_map/panel_points/all_to_all | solution.py:386
  17.8 47.2 %copy-start.2 = (bf16[64,1000]{1,0:T(8,128)(2,1)S(1)}, bf16[64,1000]{1,0:T(8,128)(2,1)}, u32[]{:S(2)}) copy-start(bf16[64,1000]{1,0:T(8,128)(2,1)} %reg.3) | copy-start | bytes 384004
  22.9 69.1 %copy-start = (bf16[1024,1000]{1,0:T(8,128)(2,1)}, bf16[1024,1000]{1,0:T(8,128)(2,1)S(1)}, u32[]{:S(2)}) copy-start(bf16[1024,1000]{1,0:T(8,128)(2,1)S(1)} %copy.12.env) | copy-start | bytes 6144004
  68.4 0.9 copy-start.4
  69.3 0.7 copy-start.5
  70.0 0.7 copy-start.6
  70.7 34.0 %all-to-all-start.1 = ((f32[32,8,256]{2,1,0:T(8,128)}), f32[32,8,256]{2,1,0:T(8,128)S(1)}, u32[]{:S(2)}, u32[]{:S(2)}) async-start(f32[32,8,256]{2,1,0:T(8,128)} %bitcast.11), calls=%async_computation.1 | async-start | bytes 524288 | tf_op jit(solution)/shard_map/gram/all_to_all | solution.py:401
  104.7 4.2 %collective-permute-start = (f32[128,1280]{1,0:T(8,128)}, f32[128,1280]{1,0:T(8,128)S(1)}, u32[]{:S(2)}, u32[]{:S(2)}) collective-permute-start(f32[128,1280]{1,0:T(8,128)} %get-tuple-element.19), channel_id=1, source_target_pairs={{0,16},{16,0},{32,48},{48,32},{64,80},{80,64},{96,112},{112,96},{1... | collective-permute-start | bytes 1966088 | tf_op jit(solution)/shard_map/product/ppermute | solution.py:410
  108.9 0.8 copy-start.7
  138.6 85.8 %copy-start.1 = (f32[512,1280]{1,0:T(8,128)S(1)}, f32[512,1280]{1,0:T(8,128)}, u32[]{:S(2)}) copy-start(f32[512,1280]{1,0:T(8,128)} %get-tuple-element.15.design) | copy-start | bytes 7864324
  138.6 85.8 %copy-start.3 = (s32[2]{0:T(128)S(1)}, s32[2]{0:T(128)}, u32[]{:S(2)}) copy-start(s32[2]{0:T(128)} %pad_add_fusion.place) | copy-start | bytes 28
Sparse Core Ops, SparseCore 0:
  10.1 81.8 all-gather.3

commit v5 on v4

--- a/solution.py
+++ b/solution.py
@@ -18,6 +18,8 @@
 COLS = SLOTS * PANEL
 HALF = PANEL // 2
 START = 0.95
+BLOCK = HALF // 4
+GRAM_ROWS = 8
 LANES = 128
 TILES = COLS // LANES
 LOW = 3
@@ -32,7 +34,9 @@
 VMEM_LIMIT = 40 * 1024 * 1024
 DESIGN_VMEM = 60 * 1024 * 1024
 
-SAME_CORE = [[2 * z + c for z in range(N_Z)] for c in range(2)]
+NEAR = [[2 * (4 * j + r) + c for r in range(4)] for j in range(4) for c in range(2)]
+FAR = [[2 * (4 * j + r) + c for j in range(4)] for r in range(4) for c in range(2)]
+CHIPS = [[8 * j + i for i in range(8)] for j in range(4)]
 CORE_SWAP = [(i, i ^ 1) for i in range(2 * N_Z)]
 
 
@@ -105,7 +109,7 @@
     hi, lo = halves(rows_ref[...])
     left = panel_hi[...]
     product = nn(left, hi) + nn(left, lo) + nn(panel_lo[...], hi)
-    product = product.reshape(N_Z, 2, HALF // N_Z, COLS)
+    product = product.reshape(4, 2, BLOCK, COLS)
     first = place[0] == 0
     keep_ref[...] = jnp.where(first, product[:, 0], product[:, 1]).reshape(HALF, COLS)
     send_ref[...] = jnp.where(first, product[:, 1], product[:, 0]).reshape(HALF, COLS)
@@ -179,49 +183,69 @@
         code_ref[:, tile_of(TILES + k)] = (low[k] - 32768).astype(jnp.int16)
 
 
-def sum_kernel(code, pieces, code_ref):
+def quarter_sums(code):
     low = [unsigned(code[:, tile_of(TILES + k)]) for k in range(LOW)]
-
-    def total(t):
+    tiles = []
+    for t in range(TILES):
         x = decode(code[:, tile_of(t)], low[t // 4], 4 * (t % 4), low[-1], t)
-        return jnp.sum(x.reshape(N_Z, HALF // N_Z, LANES), 0)
-
-    out, lane = encode([total(t) for t in range(TILES)], code_ref)
+        tiles.append(jnp.sum(x.reshape(4, BLOCK, LANES), 0))
+    return tiles
+
+
+def near_kernel(code, pieces, code_ref):
+    out, lane = encode(quarter_sums(code), code_ref)
+    rest = jnp.zeros((BLOCK - GRAM_ROWS, LANES), jnp.int32)
     gram = jnp.sum(pieces[...], 0)
-    gram_low = jnp.zeros((HALF // N_Z, LANES), jnp.int32)
+    gram_low = jnp.zeros((GRAM_ROWS, LANES), jnp.int32)
     for g in range(2):
         rounded, exponent = fixed_point(gram[:, tile_of(g)], GRAM_FIXED)
-        code_ref[:, tile_of(TILES + LOW + 1 + g)] = (rounded >> 8).astype(jnp.int16)
+        high = jnp.concatenate([rounded >> 8, rest], 0)
+        code_ref[:, tile_of(GRAM_LOW + 1 + g)] = high.astype(jnp.int16)
         gram_low = gram_low + ((rounded & 255) << (8 * g))
-        out[-1] = out[-1] + jnp.where(lane == TILES + g, exponent << 8, 0)
+        exponents = jnp.where(lane[:GRAM_ROWS] == TILES + g, exponent << 8, 0)
+        out[-1] = out[-1] + jnp.concatenate([exponents, rest], 0)
     for k in range(LOW):
         code_ref[:, tile_of(TILES + k)] = (out[k] - 32768).astype(jnp.int16)
-    code_ref[:, tile_of(GRAM_LOW)] = (gram_low - 32768).astype(jnp.int16)
+    code_ref[:, tile_of(GRAM_LOW)] = (jnp.concatenate([gram_low, rest], 0) - 32768).astype(jnp.int16)
+
+
+def far_kernel(code, code_ref):
+    out, lane = encode(quarter_sums(code), code_ref)
+
+    def gram_rows(x):
+        return jnp.concatenate([x[BLOCK * j : BLOCK * j + GRAM_ROWS] for j in range(4)], 0)
+
+    for k in range(3):
+        tile = tile_of(GRAM_LOW + k)
+        code_ref[:, tile] = gram_rows(code[:, tile].astype(jnp.int32)).astype(jnp.int16)
+    exponents = gram_rows((unsigned(code[:, tile_of(TILES + LOW - 1)]) >> 8) << 8)
+    out[-1] = out[-1] + jnp.where((lane == TILES) | (lane == TILES + 1), exponents, 0)
+    for k in range(LOW):
+        code_ref[:, tile_of(TILES + k)] = (out[k] - 32768).astype(jnp.int16)
 
 
 def code_step(keep, received):
-    half = pl.BlockSpec((HALF, COLS), lambda t: (0, 0))
+    vmem = pl.BlockSpec(memory_space=pltpu.VMEM)
     return pl.pallas_call(
         code_kernel,
-        grid=(1,),
-        in_specs=[half, half],
-        out_specs=pl.BlockSpec((HALF, CODE), lambda t: (0, 0)),
+        in_specs=[vmem, vmem],
+        out_specs=vmem,
         out_shape=jax.ShapeDtypeStruct((HALF, CODE), jnp.int16),
-        compiler_params=pltpu.CompilerParams(vmem_limit_bytes=DESIGN_VMEM),
+        compiler_params=pltpu.CompilerParams(vmem_limit_bytes=VMEM_LIMIT),
         name="code",
     )(keep, received)
 
 
-def sum_step(code, pieces):
+def sum_step(kernel, *arrays):
     vmem = pl.BlockSpec(memory_space=pltpu.VMEM)
     return pl.pallas_call(
-        sum_kernel,
-        in_specs=[vmem, vmem],
+        kernel,
+        in_specs=[vmem] * len(arrays),
         out_specs=vmem,
-        out_shape=jax.ShapeDtypeStruct((HALF // N_Z, WIDE), jnp.int16),
+        out_shape=jax.ShapeDtypeStruct((BLOCK, WIDE), jnp.int16),
         compiler_params=pltpu.CompilerParams(vmem_limit_bytes=VMEM_LIMIT),
         name="sum",
-    )(code, pieces)
+    )(*arrays)
 
 
 FULL = dict(precision=lax.Precision.HIGHEST, preferred_element_type=jnp.float32)
@@ -397,7 +421,8 @@
     )
 
     with jax.named_scope("gram"):
-        pieces = gram.reshape(2 * N_Z, HALF // N_Z, PANEL)
+        pieces = gram.reshape(4, 2, 4, GRAM_ROWS, PANEL).transpose(2, 0, 1, 3, 4)
+        pieces = pieces.reshape(2 * N_Z, GRAM_ROWS, PANEL)
         pieces = lax.all_to_all(pieces, "env", 0, 0)
 
     points = gathered.reshape(COLS, DESC)
@@ -408,10 +433,12 @@
     with jax.named_scope("product"):
         send, pieces = lax.optimization_barrier((send, pieces))
         code = code_step(keep, lax.ppermute(send, "env", CORE_SWAP))
-        code = code.reshape(N_Z, HALF // N_Z, CODE)
-        code = lax.all_to_all(code, "env", 0, 0, axis_index_groups=SAME_CORE)
-        code = sum_step(code.reshape(HALF, CODE), pieces)
-        code = lax.all_gather(code, "env", axis=0, tiled=True)
+        code = code.reshape(4, BLOCK, CODE)
+        code = lax.all_to_all(code, "env", 0, 0, axis_index_groups=NEAR)
+        code = sum_step(near_kernel, code.reshape(HALF, CODE), pieces)
+        code = lax.all_gather(code, "env", axis=0, tiled=True, axis_index_groups=FAR)
+        code = sum_step(far_kernel, code)
+        code = lax.all_gather(code, "env", axis=0, tiled=True, axis_index_groups=CHIPS)
 
     return update_step(place, design, code, factor_step(code), panel)
 

time: 239 us -> 231 us (0.967)
  blocking collectives: 106 us -> 99.8 us
  Pallas kernels: 70.7 us -> 66.5 us
    all_to_all x1, blocking collectives: 26.1 us -> 15.2 us  [shards(): code = lax.all_to_all(code, 'env', 0, 0, axis_index_groups=NEAR)]
    all_gather x1 -> x2, blocking collectives: 40 us -> 44.7 us  [the longest x1 24.6 us: shards(): lax.all_gather(code, 'env', axis=0, tiled=True, axis_index_groups=FAR)]
  transfers between devices with their start and end apart: 4 -> 4, of which waited for: 3 -> 3; matrix products, arithmetic and copies ran while one was open for 3% -> 4% of each run, Pallas kernels for 7% -> 7%
where the time goes in v5:
time: 231 us; the launch traced here: 228 us
  blocking collectives  99.8 us (43%)
  Pallas kernels  66.5 us (29%)
  waiting for transfers between devices  19.3 us (8%)
  starting transfers between devices  16.9 us (7%)
  between operations  14.9 us (6%)
  local copies, waits for them, and re-layouts  9.24 us (4%)
    pallas_call x1, Pallas kernels, factor_step(): pl.pallas_call(factor_kernel, grid=(1,), in_specs=[pl.BlockSpec((PANEL, P...  45.4 us
    all_gather x1, blocking collectives, shards(): panel_points = lax.all_gather(mine, 'env', axis=0, tiled=True)  39.8 us
    all_gather x1, blocking collectives, shards(): lax.all_gather(code, 'env', axis=0, tiled=True, axis_index_groups=FAR)  24.6 us
    all_gather x1, blocking collectives, shards(): lax.all_gather(code, 'env', axis=0, tiled=True, axis_index_groups=CHIPS)  20.1 us
    all_to_all x1, blocking collectives, shards(): code = lax.all_to_all(code, 'env', 0, 0, axis_index_groups=NEAR)  15.2 us
    all_gather x1, waiting for transfers between devices, shards(): gathered = lax.all_gather(sparse_desc, 'env', axis=1, tiled=True)  14.4 us
    pallas_call x1, Pallas kernels, design_step(): pl.pallas_call(design_kernel, grid_spec=pltpu.PrefetchScalarGridSpec(num_...  12.7 us
    all_to_all x1, starting transfers between devices, shards(): offered = lax.all_to_all(offered, 'sp', 0, 0)  7.72 us
  transfers between devices with their start and end apart: 4, of which 3 were waited for; matrix products, arithmetic and copies ran while one was open for 4% of the time, Pallas kernels for 7%

profile of v5, /device:TPU:1, one launch (start us, length us, event | category | flops | bytes accessed | tf_op | source)
XLA Modules:
  0.0 228.4 jit_solution(15742367780629779331)
XLA Ops:
  7.2 0.7 all-gather.4.cloned.1.call-update
  8.6 0.7 dynamic-slice_bitcast_fusion
  9.3 0.7 broadcast_in_dim.17
  10.0 7.7 %all-to-all-start = ((bf16[16,8,1000]{2,1,0:T(8,128)(2,1)}), bf16[16,8,1000]{2,1,0:T(8,128)(2,1)S(1)}, u32[]{:S(2)}, u32[]{:S(2)}) async-start(bf16[16,8,1000]{2,1,0:T(8,128)(2,1)} %broadcast_in_dim.17), calls=%async_computation | async-start | bytes 524288 | tf_op jit(solution)/shard_map/panel_points/all_to_all | solution.py:410
  17.8 0.7 pad_bitcast_fusion
  18.5 0.3 reduce-window.9
  18.9 0.1 slice_reduce_fusion
  19.1 0.7 fusion
  19.8 0.1 copy.11.starts
  19.9 0.1 copy.12.finish
  20.1 2.9 %copy.13.env = bf16[1024,1000]{1,0:T(8,128)(2,1)S(1)} copy(bf16[1024,1000]{0,1:T(8,128)(2,1)} %param.5) | data formatting | bytes 4096000 | tf_op args[0]
  23.0 2.2 all-to-all-done
  25.2 39.8 %all-gather = bf16[1,256,1000]{2,1,0:T(8,128)(2,1)S(1)} all-gather(bf16[1,8,1000]{2,1,0:T(8,128)(2,1)S(1)} %constant_dynamic-slice_fusion), channel_id=2, replica_groups=mesh['env'=32,'sp'=16] {'env'}, dimensions={1}, use_global_device_ids=true | all-gather | bytes 528000 | tf_op jit(solution)/shard_map/panel_points/all_gather | solution.py:412
  65.0 2.7 %panel.1 = (f32[512,256]{1,0:T(8,128)S(1)}, bf16[256,512]{1,0:T(8,128)(2,1)S(1)}, bf16[256,512]{1,0:T(8,128)(2,1)S(1)}, f32[256,256]{1,0:T(8,128)S(1)}, bf16[448,1024]{1,0:T(8,128)(2,1)S(1)}) custom-call(bf16[256,1000]{1,0:T(8,128)(2,1)S(1)} %bitcast.21, bf16[1024,1000]{1,0:T(8,128)(2,1)S(1)} %copy.13.env, bf16[64,1000]{1,0:T(8,128)(2,1)S(1)} %copy-done.3, ...), custom_call_target="tpu_custom_call" | custom-call | tf_op jit(solution)/shard_map/panel/pallas_call | solution.py:85
  67.7 0.9 copy-done.5
  68.7 0.8 copy.15
  69.5 7.0 %all-to-all-start.1 = ((f32[32,8,256]{2,1,0:T(8,128)}), f32[32,8,256]{2,1,0:T(8,128)S(1)}, u32[]{:S(2)}, u32[]{:S(2)}) async-start(f32[32,8,256]{2,1,0:T(8,128)} %bitcast.13), calls=%async_computation.1 | async-start | bytes 524288 | tf_op jit(solution)/shard_map/gram/all_to_all | solution.py:426
  76.6 0.8 copy.14.inverse
  77.4 0.6 pad_add_fusion.place
  78.0 14.4 %all-gather.4.cloned.1.call-done = bf16[5,256,1000]{2,1,0:T(8,128)(2,1)} async-done(((bf16[5,8,1000]{2,1,0:T(8,128)(2,1)}), bf16[5,256,1000]{2,1,0:T(8,128)(2,1)}) %all-gather.4.cloned.1.call-update) | async-done | bytes 2560016 | tf_op jit(solution)/shard_map/all_gather | solution.py:405
  92.4 12.7 %design.1 = (f32[512,1280]{1,0:T(8,128)}, f32[128,1280]{1,0:T(8,128)}, f32[128,1280]{1,0:T(8,128)}) custom-call(s32[2]{0:T(128)} %pad_add_fusion.place, bf16[1280,1000]{1,0:T(8,128)(2,1)} %bitcast.29, bf16[1024,1000]{1,0:T(8,128)(2,1)} %copy-done, bf16[64,1000]{1,0:T(8,128)(2,1)} %reg.3, bf16[448,1024]{1,0:T(8,128)(2,1)} %copy-done.5, ...), custom_call_target="tpu_custom_call" | custom-call | flops 7000000000 | bytes 9000000 | tf_op jit(solution)/shard_map/design/pallas_call | solution.py:122
  105.2 2.2 collective-permute-start
  107.4 2.0 collective-permute-done.received
  109.4 1.1 copy-done.2
  110.5 0.7 code.1
  111.2 15.2 %all_to_all.15 = s16[4,32,1664]{2,1,0:T(8,128)(2,1)S(1)} all-to-all(s16[4,32,1664]{2,1,0:T(8,128)(2,1)S(1)} %bitcast.23), channel_id=1, replica_groups={{0,32,64,96},{16,48,80,112},{128,160,192,224},{144,176,208,240},{256,28..., dimensions={0} | all-to-all | bytes 851968 | tf_op jit(solution)/shard_map/product/all_to_all | solution.py:437
  126.4 0.5 sum.2
  126.9 24.6 %all_gather.14.code = s16[128,2048]{1,0:T(8,128)(2,1)S(1)} all-gather(s16[32,2048]{1,0:T(8,128)(2,1)S(1)} %sum.2), channel_id=1, replica_groups={{0,128,256,384},{16,144,272,400},{32,160,288,416},{48,176,304,432},{64,..., dimensions={0}, use_global_device_ids=true | all-gather | bytes 655360 | tf_op jit(solution)/shard_map/product/all_gather | solution.py:439
  151.5 0.5 sum.3
  151.9 20.1 %all-gather.5.high.low.exponents = s16[256,2048]{1,0:T(8,128)(2,1)S(1)} all-gather(s16[32,2048]{1,0:T(8,128)(2,1)S(1)} %sum.3), channel_id=1, replica_groups={{0,16,32,48,64,80,96,112},{128,144,160,176,192,208,224,240},{256,272,28..., dimensions={0}, use_global_device_ids=true | all-gather | bytes 1179648 | tf_op jit(solution)/shard_map/product/all_gather | solution.py:441
  172.0 45.4 %factor.1.inverse_factor = f32[256,256]{1,0:T(8,128)S(1)} custom-call(s16[256,2048]{1,0:T(8,128)(2,1)S(1)} %all-gather.5.high.low.exponents, s16[256,2048]{1,0:T(8,128)(2,1)S(1)} %all-gather.5.high.low.exponents, s16[256,2048]{1,0:T(8,128)(2,1)S(1)} %all-gather.5.high.low.exponents), custom_call_target="tpu_custom_call" | custom-call | tf_op jit(solution)/shard_map/factor/pallas_call | solution.py:320
  217.4 4.1 %update.1 = (f32[512,1280]{1,0:T(8,128)}, f32[256,1280]{1,0:T(8,128)}) custom-call(s32[2]{0:T(128)S(1)} %copy-done.4, f32[512,1280]{1,0:T(8,128)S(1)} %copy-done.1, s16[256,2048]{1,0:T(8,128)(2,1)S(1)} %all-gather.5.high.low.exponents, s16[256,2048]{1,0:T(8,128)(2,1)S(1)} %all-gather.5.high.low.exponents, s16[256,2048]{1,0:T(8,128)(2,1)S(1)} %all-gather.5.high.low.exponents, ...), custom_call_target="tpu_custom_call" | custom-call | tf_op jit(solution)/shard_map/update/pallas_call | solution.py:372
  (24 shorter events, 0.4 us)
Async XLA Ops:
  7.2 85.3 %all-gather.4.cloned.1.call-start = ((), (), s32[]{:S(2)}) async-start(), calls=%async_computation.3 | async-start | bytes 2703360 | tf_op jit(solution)/shard_map/all_gather | solution.py:405
  10.0 12.9 %copy-start.8 = (s32[1,448]{1,0:T(1,128)S(1)}, s32[1,448]{1,0:T(1,128)}, u32[]{:S(2)}) copy-start(s32[1,448]{1,0:T(1,128)} %param.6) | copy-start | bytes 5380
  10.0 15.1 %all-to-all-start = ((bf16[16,8,1000]{2,1,0:T(8,128)(2,1)}), bf16[16,8,1000]{2,1,0:T(8,128)(2,1)S(1)}, u32[]{:S(2)}, u32[]{:S(2)}) async-start(bf16[16,8,1000]{2,1,0:T(8,128)(2,1)} %broadcast_in_dim.17), calls=%async_computation | async-start | bytes 524288 | tf_op jit(solution)/shard_map/panel_points/all_to_all | solution.py:410
  17.8 47.2 %copy-start.3 = (bf16[64,1000]{1,0:T(8,128)(2,1)S(1)}, bf16[64,1000]{1,0:T(8,128)(2,1)}, u32[]{:S(2)}) copy-start(bf16[64,1000]{1,0:T(8,128)(2,1)} %reg.3) | copy-start | bytes 384004
  22.9 69.5 %copy-start = (bf16[1024,1000]{1,0:T(8,128)(2,1)}, bf16[1024,1000]{1,0:T(8,128)(2,1)S(1)}, u32[]{:S(2)}) copy-start(bf16[1024,1000]{1,0:T(8,128)(2,1)S(1)} %copy.13.env) | copy-start | bytes 6144004
  67.7 0.9 copy-start.5
  68.6 0.8 copy-start.6
  68.6 0.9 copy-start.7
  69.5 35.6 %all-to-all-start.1 = ((f32[32,8,256]{2,1,0:T(8,128)}), f32[32,8,256]{2,1,0:T(8,128)S(1)}, u32[]{:S(2)}, u32[]{:S(2)}) async-start(f32[32,8,256]{2,1,0:T(8,128)} %bitcast.13), calls=%async_computation.1 | async-start | bytes 524288 | tf_op jit(solution)/shard_map/gram/all_to_all | solution.py:426
  105.2 4.2 %collective-permute-start = (f32[128,1280]{1,0:T(8,128)}, f32[128,1280]{1,0:T(8,128)S(1)}, u32[]{:S(2)}, u32[]{:S(2)}) collective-permute-start(f32[128,1280]{1,0:T(8,128)} %get-tuple-element.19), channel_id=1, source_target_pairs={{0,16},{16,0},{32,48},{48,32},{64,80},{80,64},{96,112},{112,96},{1... | collective-permute-start | bytes 1966088 | tf_op jit(solution)/shard_map/product/ppermute | solution.py:435
  109.4 1.1 copy-start.2
  151.5 66.0 %copy-start.1 = (f32[512,1280]{1,0:T(8,128)S(1)}, f32[512,1280]{1,0:T(8,128)}, u32[]{:S(2)}) copy-start(f32[512,1280]{1,0:T(8,128)} %get-tuple-element.15.design) | copy-start | bytes 7864324
  151.5 66.0 %copy-start.4 = (s32[2]{0:T(128)S(1)}, s32[2]{0:T(128)}, u32[]{:S(2)}) copy-start(s32[2]{0:T(128)} %pad_add_fusion.place) | copy-start | bytes 28
Sparse Core Ops, SparseCore 0:
  10.1 82.2 all-gather.3

commit v6 on v5

--- a/solution.py
+++ b/solution.py
@@ -196,29 +196,31 @@
     out, lane = encode(quarter_sums(code), code_ref)
     rest = jnp.zeros((BLOCK - GRAM_ROWS, LANES), jnp.int32)
     gram = jnp.sum(pieces[...], 0)
+    groups = []
     gram_low = jnp.zeros((GRAM_ROWS, LANES), jnp.int32)
     for g in range(2):
         rounded, exponent = fixed_point(gram[:, tile_of(g)], GRAM_FIXED)
-        high = jnp.concatenate([rounded >> 8, rest], 0)
-        code_ref[:, tile_of(GRAM_LOW + 1 + g)] = high.astype(jnp.int16)
+        groups.append(rounded >> 8)
         gram_low = gram_low + ((rounded & 255) << (8 * g))
         exponents = jnp.where(lane[:GRAM_ROWS] == TILES + g, exponent << 8, 0)
         out[-1] = out[-1] + jnp.concatenate([exponents, rest], 0)
     for k in range(LOW):
         code_ref[:, tile_of(TILES + k)] = (out[k] - 32768).astype(jnp.int16)
-    code_ref[:, tile_of(GRAM_LOW)] = (jnp.concatenate([gram_low, rest], 0) - 32768).astype(jnp.int16)
+    groups = [gram_low - 32768] + groups + [rest[:GRAM_ROWS]]
+    code_ref[:, tile_of(GRAM_LOW)] = jnp.concatenate(groups, 0).astype(jnp.int16)
 
 
 def far_kernel(code, code_ref):
     out, lane = encode(quarter_sums(code), code_ref)
 
-    def gram_rows(x):
-        return jnp.concatenate([x[BLOCK * j : BLOCK * j + GRAM_ROWS] for j in range(4)], 0)
+    def gram_rows(x, k):
+        first = [BLOCK * j + GRAM_ROWS * k for j in range(4)]
+        return jnp.concatenate([x[i : i + GRAM_ROWS] for i in first], 0)
 
     for k in range(3):
-        tile = tile_of(GRAM_LOW + k)
-        code_ref[:, tile] = gram_rows(code[:, tile].astype(jnp.int32)).astype(jnp.int16)
-    exponents = gram_rows((unsigned(code[:, tile_of(TILES + LOW - 1)]) >> 8) << 8)
+        tile = code[:, tile_of(GRAM_LOW)].astype(jnp.int32)
+        code_ref[:, tile_of(GRAM_LOW + k)] = gram_rows(tile, k).astype(jnp.int16)
+    exponents = gram_rows((unsigned(code[:, tile_of(TILES + LOW - 1)]) >> 8) << 8, 0)
     out[-1] = out[-1] + jnp.where((lane == TILES) | (lane == TILES + 1), exponents, 0)
     for k in range(LOW):
         code_ref[:, tile_of(TILES + k)] = (out[k] - 32768).astype(jnp.int16)
@@ -236,13 +238,13 @@
     )(keep, received)
 
 
-def sum_step(kernel, *arrays):
+def sum_step(kernel, width, *arrays):
     vmem = pl.BlockSpec(memory_space=pltpu.VMEM)
     return pl.pallas_call(
         kernel,
         in_specs=[vmem] * len(arrays),
         out_specs=vmem,
-        out_shape=jax.ShapeDtypeStruct((BLOCK, WIDE), jnp.int16),
+        out_shape=jax.ShapeDtypeStruct((BLOCK, width), jnp.int16),
         compiler_params=pltpu.CompilerParams(vmem_limit_bytes=VMEM_LIMIT),
         name="sum",
     )(*arrays)
@@ -435,9 +437,9 @@
         code = code_step(keep, lax.ppermute(send, "env", CORE_SWAP))
         code = code.reshape(4, BLOCK, CODE)
         code = lax.all_to_all(code, "env", 0, 0, axis_index_groups=NEAR)
-        code = sum_step(near_kernel, code.reshape(HALF, CODE), pieces)
+        code = sum_step(near_kernel, CODE + LANES, code.reshape(HALF, CODE), pieces)
         code = lax.all_gather(code, "env", axis=0, tiled=True, axis_index_groups=FAR)
-        code = sum_step(far_kernel, code)
+        code = sum_step(far_kernel, WIDE, code)
         code = lax.all_gather(code, "env", axis=0, tiled=True, axis_index_groups=CHIPS)
 
     return update_step(place, design, code, factor_step(code), panel)

time: 231 us -> 229 us (level)
  blocking collectives: 99.8 us -> 96.6 us
where the time goes in v6:
time: 229 us; the launch traced here: 225 us
  blocking collectives  96.6 us (42%)
  Pallas kernels  66.5 us (29%)
  waiting for transfers between devices  19.3 us (8%)
  starting transfers between devices  16.9 us (7%)
  between operations  14.9 us (7%)
  local copies, waits for them, and re-layouts  9.24 us (4%)
    pallas_call x1, Pallas kernels, factor_step(): pl.pallas_call(factor_kernel, grid=(1,), in_specs=[pl.BlockSpec((PANEL, P...  45.4 us
    all_gather x1, blocking collectives, shards(): panel_points = lax.all_gather(mine, 'env', axis=0, tiled=True)  39.8 us
    all_gather x1, blocking collectives, shards(): lax.all_gather(code, 'env', axis=0, tiled=True, axis_index_groups=FAR)  23.3 us
    all_gather x1, blocking collectives, shards(): lax.all_gather(code, 'env', axis=0, tiled=True, axis_index_groups=CHIPS)  18.2 us
    all_to_all x1, blocking collectives, shards(): code = lax.all_to_all(code, 'env', 0, 0, axis_index_groups=NEAR)  15.2 us
    all_gather x1, waiting for transfers between devices, shards(): gathered = lax.all_gather(sparse_desc, 'env', axis=1, tiled=True)  14.4 us
    pallas_call x1, Pallas kernels, design_step(): pl.pallas_call(design_kernel, grid_spec=pltpu.PrefetchScalarGridSpec(num_...  12.7 us
    all_to_all x1, starting transfers between devices, shards(): offered = lax.all_to_all(offered, 'sp', 0, 0)  7.72 us
  transfers between devices with their start and end apart: 4, of which 3 were waited for; matrix products, arithmetic and copies ran while one was open for 4% of the time, Pallas kernels for 7%

profile of v6, /device:TPU:1, one launch (start us, length us, event | category | flops | bytes accessed | tf_op | source)
XLA Modules:
  0.0 225.2 jit_solution(5711704615671450883)
XLA Ops:
  7.2 0.7 all-gather.4.cloned.1.call-update
  8.6 0.7 dynamic-slice_bitcast_fusion
  9.3 0.7 broadcast_in_dim.17
  10.0 7.7 %all-to-all-start = ((bf16[16,8,1000]{2,1,0:T(8,128)(2,1)}), bf16[16,8,1000]{2,1,0:T(8,128)(2,1)S(1)}, u32[]{:S(2)}, u32[]{:S(2)}) async-start(bf16[16,8,1000]{2,1,0:T(8,128)(2,1)} %broadcast_in_dim.17), calls=%async_computation | async-start | bytes 524288 | tf_op jit(solution)/shard_map/panel_points/all_to_all | solution.py:412
  17.8 0.7 pad_bitcast_fusion
  18.5 0.3 reduce-window.9
  18.9 0.1 slice_reduce_fusion
  19.1 0.7 fusion
  19.8 0.1 copy.11.starts
  19.9 0.1 copy.12.finish
  20.1 2.9 %copy.13.env = bf16[1024,1000]{1,0:T(8,128)(2,1)S(1)} copy(bf16[1024,1000]{0,1:T(8,128)(2,1)} %param.5) | data formatting | bytes 4096000 | tf_op args[0]
  23.0 2.2 all-to-all-done
  25.2 39.8 %all-gather = bf16[1,256,1000]{2,1,0:T(8,128)(2,1)S(1)} all-gather(bf16[1,8,1000]{2,1,0:T(8,128)(2,1)S(1)} %constant_dynamic-slice_fusion), channel_id=2, replica_groups=mesh['env'=32,'sp'=16] {'env'}, dimensions={1}, use_global_device_ids=true | all-gather | bytes 528000 | tf_op jit(solution)/shard_map/panel_points/all_gather | solution.py:414
  65.0 2.7 %panel.1 = (f32[512,256]{1,0:T(8,128)S(1)}, bf16[256,512]{1,0:T(8,128)(2,1)S(1)}, bf16[256,512]{1,0:T(8,128)(2,1)S(1)}, f32[256,256]{1,0:T(8,128)S(1)}, bf16[448,1024]{1,0:T(8,128)(2,1)S(1)}) custom-call(bf16[256,1000]{1,0:T(8,128)(2,1)S(1)} %bitcast.21, bf16[1024,1000]{1,0:T(8,128)(2,1)S(1)} %copy.13.env, bf16[64,1000]{1,0:T(8,128)(2,1)S(1)} %copy-done.3, ...), custom_call_target="tpu_custom_call" | custom-call | tf_op jit(solution)/shard_map/panel/pallas_call | solution.py:85
  67.7 0.9 copy-done.5
  68.7 0.8 copy.15
  69.5 7.0 %all-to-all-start.1 = ((f32[32,8,256]{2,1,0:T(8,128)}), f32[32,8,256]{2,1,0:T(8,128)S(1)}, u32[]{:S(2)}, u32[]{:S(2)}) async-start(f32[32,8,256]{2,1,0:T(8,128)} %bitcast.13), calls=%async_computation.1 | async-start | bytes 524288 | tf_op jit(solution)/shard_map/gram/all_to_all | solution.py:428
  76.6 0.8 copy.14.inverse
  77.4 0.6 pad_add_fusion.place
  78.0 14.4 %all-gather.4.cloned.1.call-done = bf16[5,256,1000]{2,1,0:T(8,128)(2,1)} async-done(((bf16[5,8,1000]{2,1,0:T(8,128)(2,1)}), bf16[5,256,1000]{2,1,0:T(8,128)(2,1)}) %all-gather.4.cloned.1.call-update) | async-done | bytes 2560016 | tf_op jit(solution)/shard_map/all_gather | solution.py:407
  92.4 12.7 %design.1 = (f32[512,1280]{1,0:T(8,128)}, f32[128,1280]{1,0:T(8,128)}, f32[128,1280]{1,0:T(8,128)}) custom-call(s32[2]{0:T(128)} %pad_add_fusion.place, bf16[1280,1000]{1,0:T(8,128)(2,1)} %bitcast.29, bf16[1024,1000]{1,0:T(8,128)(2,1)} %copy-done, bf16[64,1000]{1,0:T(8,128)(2,1)} %reg.3, bf16[448,1024]{1,0:T(8,128)(2,1)} %copy-done.5, ...), custom_call_target="tpu_custom_call" | custom-call | flops 7000000000 | bytes 9000000 | tf_op jit(solution)/shard_map/design/pallas_call | solution.py:122
  105.2 2.2 collective-permute-start
  107.4 2.0 collective-permute-done.received
  109.4 1.1 copy-done.2
  110.5 0.7 code.1
  111.2 15.2 %all_to_all.15 = s16[4,32,1664]{2,1,0:T(8,128)(2,1)S(1)} all-to-all(s16[4,32,1664]{2,1,0:T(8,128)(2,1)S(1)} %bitcast.23), channel_id=1, replica_groups={{0,32,64,96},{16,48,80,112},{128,160,192,224},{144,176,208,240},{256,28..., dimensions={0} | all-to-all | bytes 851968 | tf_op jit(solution)/shard_map/product/all_to_all | solution.py:439
  126.4 0.5 sum.2
  126.9 23.3 %all_gather.14.code = s16[128,1792]{1,0:T(8,128)(2,1)S(1)} all-gather(s16[32,1792]{1,0:T(8,128)(2,1)S(1)} %sum.2), channel_id=1, replica_groups={{0,128,256,384},{16,144,272,400},{32,160,288,416},{48,176,304,432},{64,..., dimensions={0}, use_global_device_ids=true | all-gather | bytes 573440 | tf_op jit(solution)/shard_map/product/all_gather | solution.py:441
  150.1 0.5 sum.3
  150.6 18.2 %all-gather.5.high.low.exponents = s16[256,2048]{1,0:T(8,128)(2,1)S(1)} all-gather(s16[32,2048]{1,0:T(8,128)(2,1)S(1)} %sum.3), channel_id=1, replica_groups={{0,16,32,48,64,80,96,112},{128,144,160,176,192,208,224,240},{256,272,28..., dimensions={0}, use_global_device_ids=true | all-gather | bytes 1179648 | tf_op jit(solution)/shard_map/product/all_gather | solution.py:443
  168.8 45.4 %factor.1.inverse_factor = f32[256,256]{1,0:T(8,128)S(1)} custom-call(s16[256,2048]{1,0:T(8,128)(2,1)S(1)} %all-gather.5.high.low.exponents, s16[256,2048]{1,0:T(8,128)(2,1)S(1)} %all-gather.5.high.low.exponents, s16[256,2048]{1,0:T(8,128)(2,1)S(1)} %all-gather.5.high.low.exponents), custom_call_target="tpu_custom_call" | custom-call | tf_op jit(solution)/shard_map/factor/pallas_call | solution.py:322
  214.2 4.1 %update.1 = (f32[512,1280]{1,0:T(8,128)}, f32[256,1280]{1,0:T(8,128)}) custom-call(s32[2]{0:T(128)S(1)} %copy-done.4, f32[512,1280]{1,0:T(8,128)S(1)} %copy-done.1, s16[256,2048]{1,0:T(8,128)(2,1)S(1)} %all-gather.5.high.low.exponents, s16[256,2048]{1,0:T(8,128)(2,1)S(1)} %all-gather.5.high.low.exponents, s16[256,2048]{1,0:T(8,128)(2,1)S(1)} %all-gather.5.high.low.exponents, ...), custom_call_target="tpu_custom_call" | custom-call | tf_op jit(solution)/shard_map/update/pallas_call | solution.py:374
  (24 shorter events, 0.4 us)
Async XLA Ops:
  7.2 85.3 %all-gather.4.cloned.1.call-start = ((), (), s32[]{:S(2)}) async-start(), calls=%async_computation.3 | async-start | bytes 2703360 | tf_op jit(solution)/shard_map/all_gather | solution.py:407
  10.0 12.9 %copy-start.8 = (s32[1,448]{1,0:T(1,128)S(1)}, s32[1,448]{1,0:T(1,128)}, u32[]{:S(2)}) copy-start(s32[1,448]{1,0:T(1,128)} %param.6) | copy-start | bytes 5380
  10.0 15.1 %all-to-all-start = ((bf16[16,8,1000]{2,1,0:T(8,128)(2,1)}), bf16[16,8,1000]{2,1,0:T(8,128)(2,1)S(1)}, u32[]{:S(2)}, u32[]{:S(2)}) async-start(bf16[16,8,1000]{2,1,0:T(8,128)(2,1)} %broadcast_in_dim.17), calls=%async_computation | async-start | bytes 524288 | tf_op jit(solution)/shard_map/panel_points/all_to_all | solution.py:412
  17.8 47.2 %copy-start.3 = (bf16[64,1000]{1,0:T(8,128)(2,1)S(1)}, bf16[64,1000]{1,0:T(8,128)(2,1)}, u32[]{:S(2)}) copy-start(bf16[64,1000]{1,0:T(8,128)(2,1)} %reg.3) | copy-start | bytes 384004
  22.9 69.5 %copy-start = (bf16[1024,1000]{1,0:T(8,128)(2,1)}, bf16[1024,1000]{1,0:T(8,128)(2,1)S(1)}, u32[]{:S(2)}) copy-start(bf16[1024,1000]{1,0:T(8,128)(2,1)S(1)} %copy.13.env) | copy-start | bytes 6144004
  67.7 0.9 copy-start.5
  68.6 0.8 copy-start.6
  68.6 0.9 copy-start.7
  69.5 35.6 %all-to-all-start.1 = ((f32[32,8,256]{2,1,0:T(8,128)}), f32[32,8,256]{2,1,0:T(8,128)S(1)}, u32[]{:S(2)}, u32[]{:S(2)}) async-start(f32[32,8,256]{2,1,0:T(8,128)} %bitcast.13), calls=%async_computation.1 | async-start | bytes 524288 | tf_op jit(solution)/shard_map/gram/all_to_all | solution.py:428
  105.2 4.2 %collective-permute-start = (f32[128,1280]{1,0:T(8,128)}, f32[128,1280]{1,0:T(8,128)S(1)}, u32[]{:S(2)}, u32[]{:S(2)}) collective-permute-start(f32[128,1280]{1,0:T(8,128)} %get-tuple-element.19), channel_id=1, source_target_pairs={{0,16},{16,0},{32,48},{48,32},{64,80},{80,64},{96,112},{112,96},{1... | collective-permute-start | bytes 1966088 | tf_op jit(solution)/shard_map/product/ppermute | solution.py:437
  109.4 1.1 copy-start.2
  150.1 64.1 %copy-start.1 = (f32[512,1280]{1,0:T(8,128)S(1)}, f32[512,1280]{1,0:T(8,128)}, u32[]{:S(2)}) copy-start(f32[512,1280]{1,0:T(8,128)} %get-tuple-element.15.design) | copy-start | bytes 7864324
  150.1 64.1 %copy-start.4 = (s32[2]{0:T(128)S(1)}, s32[2]{0:T(128)}, u32[]{:S(2)}) copy-start(s32[2]{0:T(128)} %pad_add_fusion.place) | copy-start | bytes 28
Sparse Core Ops, SparseCore 0:
  10.1 82.2 all-gather.3

commit v7 on v6

--- a/solution.py
+++ b/solution.py
@@ -177,7 +177,10 @@
     return number.astype(jnp.float32) * unit(exponents, t, FIXED)
 
 
-def code_kernel(keep, received, code_ref):
+def code_kernel(kept, received, code_ref, keep, sem):
+    bring = pltpu.make_async_copy(kept, keep, sem)
+    bring.start()
+    bring.wait()
     low, _ = encode([keep[:, tile_of(t)] + received[:, tile_of(t)] for t in range(TILES)], code_ref)
     for k in range(LOW):
         code_ref[:, tile_of(TILES + k)] = (low[k] - 32768).astype(jnp.int16)
@@ -230,9 +233,10 @@
     vmem = pl.BlockSpec(memory_space=pltpu.VMEM)
     return pl.pallas_call(
         code_kernel,
-        in_specs=[vmem, vmem],
+        in_specs=[pl.BlockSpec(memory_space=pl.ANY), vmem],
         out_specs=vmem,
         out_shape=jax.ShapeDtypeStruct((HALF, CODE), jnp.int16),
+        scratch_shapes=[pltpu.VMEM((HALF, COLS), jnp.float32), pltpu.SemaphoreType.DMA],
         compiler_params=pltpu.CompilerParams(vmem_limit_bytes=VMEM_LIMIT),
         name="code",
     )(keep, received)

time: 229 us -> 230 us (level)
  no operation moved by 1% of the time
where the time goes in v7:
time: 230 us; the launch traced here: 225 us
  blocking collectives  96.6 us (42%)
  Pallas kernels  66.7 us (29%)
  waiting for transfers between devices  19.3 us (8%)
  starting transfers between devices  16.9 us (7%)
  between operations  14.9 us (6%)
  local copies, waits for them, and re-layouts  9.24 us (4%)
    pallas_call x1, Pallas kernels, factor_step(): pl.pallas_call(factor_kernel, grid=(1,), in_specs=[pl.BlockSpec((PANEL, P...  45.4 us
    all_gather x1, blocking collectives, shards(): panel_points = lax.all_gather(mine, 'env', axis=0, tiled=True)  39.8 us
    all_gather x1, blocking collectives, shards(): lax.all_gather(code, 'env', axis=0, tiled=True, axis_index_groups=FAR)  23.3 us
    all_gather x1, blocking collectives, shards(): lax.all_gather(code, 'env', axis=0, tiled=True, axis_index_groups=CHIPS)  18.2 us
    all_to_all x1, blocking collectives, shards(): code = lax.all_to_all(code, 'env', 0, 0, axis_index_groups=NEAR)  15.2 us
    all_gather x1, waiting for transfers between devices, shards(): gathered = lax.all_gather(sparse_desc, 'env', axis=1, tiled=True)  14.4 us
    pallas_call x1, Pallas kernels, design_step(): pl.pallas_call(design_kernel, grid_spec=pltpu.PrefetchScalarGridSpec(num_...  12.7 us
    all_to_all x1, starting transfers between devices, shards(): offered = lax.all_to_all(offered, 'sp', 0, 0)  7.72 us
  transfers between devices with their start and end apart: 4, of which 3 were waited for; matrix products, arithmetic and copies ran while one was open for 4% of the time, Pallas kernels for 7%

profile of v7, /device:TPU:1, one launch (start us, length us, event | category | flops | bytes accessed | tf_op | source)
XLA Modules:
  0.0 225.4 jit_solution(2501961826934905121)
XLA Ops:
  7.2 0.7 all-gather.4.cloned.1.call-update
  8.6 0.7 dynamic-slice_bitcast_fusion
  9.3 0.7 broadcast_in_dim.17
  10.0 7.7 %all-to-all-start = ((bf16[16,8,1000]{2,1,0:T(8,128)(2,1)}), bf16[16,8,1000]{2,1,0:T(8,128)(2,1)S(1)}, u32[]{:S(2)}, u32[]{:S(2)}) async-start(bf16[16,8,1000]{2,1,0:T(8,128)(2,1)} %broadcast_in_dim.17), calls=%async_computation | async-start | bytes 524288 | tf_op jit(solution)/shard_map/panel_points/all_to_all | solution.py:416
  17.8 0.7 pad_bitcast_fusion
  18.5 0.3 reduce-window.9
  18.9 0.1 slice_reduce_fusion
  19.1 0.7 fusion
  19.8 0.1 copy.11.starts
  19.9 0.1 copy.12.finish
  20.1 2.9 %copy.13.env = bf16[1024,1000]{1,0:T(8,128)(2,1)S(1)} copy(bf16[1024,1000]{0,1:T(8,128)(2,1)} %param.5) | data formatting | bytes 4096000 | tf_op args[0]
  23.0 2.2 all-to-all-done
  25.2 39.8 %all-gather = bf16[1,256,1000]{2,1,0:T(8,128)(2,1)S(1)} all-gather(bf16[1,8,1000]{2,1,0:T(8,128)(2,1)S(1)} %constant_dynamic-slice_fusion), channel_id=2, replica_groups=mesh['env'=32,'sp'=16] {'env'}, dimensions={1}, use_global_device_ids=true | all-gather | bytes 528000 | tf_op jit(solution)/shard_map/panel_points/all_gather | solution.py:418
  65.0 2.7 %panel.1 = (f32[512,256]{1,0:T(8,128)S(1)}, bf16[256,512]{1,0:T(8,128)(2,1)S(1)}, bf16[256,512]{1,0:T(8,128)(2,1)S(1)}, f32[256,256]{1,0:T(8,128)S(1)}, bf16[448,1024]{1,0:T(8,128)(2,1)S(1)}) custom-call(bf16[256,1000]{1,0:T(8,128)(2,1)S(1)} %bitcast.21, bf16[1024,1000]{1,0:T(8,128)(2,1)S(1)} %copy.13.env, bf16[64,1000]{1,0:T(8,128)(2,1)S(1)} %copy-done.3, ...), custom_call_target="tpu_custom_call" | custom-call | tf_op jit(solution)/shard_map/panel/pallas_call | solution.py:85
  67.7 0.9 copy-done.5
  68.7 0.8 copy.15
  69.5 7.0 %all-to-all-start.1 = ((f32[32,8,256]{2,1,0:T(8,128)}), f32[32,8,256]{2,1,0:T(8,128)S(1)}, u32[]{:S(2)}, u32[]{:S(2)}) async-start(f32[32,8,256]{2,1,0:T(8,128)} %bitcast.13), calls=%async_computation.1 | async-start | bytes 524288 | tf_op jit(solution)/shard_map/gram/all_to_all | solution.py:432
  76.6 0.8 copy.14.inverse
  77.4 0.6 pad_add_fusion.place
  78.0 14.4 %all-gather.4.cloned.1.call-done = bf16[5,256,1000]{2,1,0:T(8,128)(2,1)} async-done(((bf16[5,8,1000]{2,1,0:T(8,128)(2,1)}), bf16[5,256,1000]{2,1,0:T(8,128)(2,1)}) %all-gather.4.cloned.1.call-update) | async-done | bytes 2560016 | tf_op jit(solution)/shard_map/all_gather | solution.py:411
  92.4 12.7 %design.1 = (f32[512,1280]{1,0:T(8,128)}, f32[128,1280]{1,0:T(8,128)}, f32[128,1280]{1,0:T(8,128)}) custom-call(s32[2]{0:T(128)} %pad_add_fusion.place, bf16[1280,1000]{1,0:T(8,128)(2,1)} %bitcast.29, bf16[1024,1000]{1,0:T(8,128)(2,1)} %copy-done, bf16[64,1000]{1,0:T(8,128)(2,1)} %reg.3, bf16[448,1024]{1,0:T(8,128)(2,1)} %copy-done.5, ...), custom_call_target="tpu_custom_call" | custom-call | flops 7000000000 | bytes 9000000 | tf_op jit(solution)/shard_map/design/pallas_call | solution.py:122
  105.2 2.2 collective-permute-start
  107.4 2.0 collective-permute-done.received
  109.4 1.1 copy-done.2
  110.5 0.9 code.1
  111.4 15.2 %all_to_all.15 = s16[4,32,1664]{2,1,0:T(8,128)(2,1)S(1)} all-to-all(s16[4,32,1664]{2,1,0:T(8,128)(2,1)S(1)} %bitcast.23), channel_id=1, replica_groups={{0,32,64,96},{16,48,80,112},{128,160,192,224},{144,176,208,240},{256,28..., dimensions={0} | all-to-all | bytes 851968 | tf_op jit(solution)/shard_map/product/all_to_all | solution.py:443
  126.6 0.5 sum.2
  127.1 23.3 %all_gather.14.code = s16[128,1792]{1,0:T(8,128)(2,1)S(1)} all-gather(s16[32,1792]{1,0:T(8,128)(2,1)S(1)} %sum.2), channel_id=1, replica_groups={{0,128,256,384},{16,144,272,400},{32,160,288,416},{48,176,304,432},{64,..., dimensions={0}, use_global_device_ids=true | all-gather | bytes 573440 | tf_op jit(solution)/shard_map/product/all_gather | solution.py:445
  150.3 0.5 sum.3
  150.8 18.2 %all-gather.5.high.low.exponents = s16[256,2048]{1,0:T(8,128)(2,1)S(1)} all-gather(s16[32,2048]{1,0:T(8,128)(2,1)S(1)} %sum.3), channel_id=1, replica_groups={{0,16,32,48,64,80,96,112},{128,144,160,176,192,208,224,240},{256,272,28..., dimensions={0}, use_global_device_ids=true | all-gather | bytes 1179648 | tf_op jit(solution)/shard_map/product/all_gather | solution.py:447
  169.1 45.4 %factor.1.inverse_factor = f32[256,256]{1,0:T(8,128)S(1)} custom-call(s16[256,2048]{1,0:T(8,128)(2,1)S(1)} %all-gather.5.high.low.exponents, s16[256,2048]{1,0:T(8,128)(2,1)S(1)} %all-gather.5.high.low.exponents, s16[256,2048]{1,0:T(8,128)(2,1)S(1)} %all-gather.5.high.low.exponents), custom_call_target="tpu_custom_call" | custom-call | tf_op jit(solution)/shard_map/factor/pallas_call | solution.py:326
  214.5 4.1 %update.1 = (f32[512,1280]{1,0:T(8,128)}, f32[256,1280]{1,0:T(8,128)}) custom-call(s32[2]{0:T(128)S(1)} %copy-done.4, f32[512,1280]{1,0:T(8,128)S(1)} %copy-done.1, s16[256,2048]{1,0:T(8,128)(2,1)S(1)} %all-gather.5.high.low.exponents, s16[256,2048]{1,0:T(8,128)(2,1)S(1)} %all-gather.5.high.low.exponents, s16[256,2048]{1,0:T(8,128)(2,1)S(1)} %all-gather.5.high.low.exponents, ...), custom_call_target="tpu_custom_call" | custom-call | tf_op jit(solution)/shard_map/update/pallas_call | solution.py:378
  (24 shorter events, 0.4 us)
Async XLA Ops:
  7.2 85.3 %all-gather.4.cloned.1.call-start = ((), (), s32[]{:S(2)}) async-start(), calls=%async_computation.3 | async-start | bytes 2703360 | tf_op jit(solution)/shard_map/all_gather | solution.py:411
  10.0 12.9 %copy-start.8 = (s32[1,448]{1,0:T(1,128)S(1)}, s32[1,448]{1,0:T(1,128)}, u32[]{:S(2)}) copy-start(s32[1,448]{1,0:T(1,128)} %param.6) | copy-start | bytes 5380
  10.0 15.1 %all-to-all-start = ((bf16[16,8,1000]{2,1,0:T(8,128)(2,1)}), bf16[16,8,1000]{2,1,0:T(8,128)(2,1)S(1)}, u32[]{:S(2)}, u32[]{:S(2)}) async-start(bf16[16,8,1000]{2,1,0:T(8,128)(2,1)} %broadcast_in_dim.17), calls=%async_computation | async-start | bytes 524288 | tf_op jit(solution)/shard_map/panel_points/all_to_all | solution.py:416
  17.8 47.2 %copy-start.3 = (bf16[64,1000]{1,0:T(8,128)(2,1)S(1)}, bf16[64,1000]{1,0:T(8,128)(2,1)}, u32[]{:S(2)}) copy-start(bf16[64,1000]{1,0:T(8,128)(2,1)} %reg.3) | copy-start | bytes 384004
  22.9 69.5 %copy-start = (bf16[1024,1000]{1,0:T(8,128)(2,1)}, bf16[1024,1000]{1,0:T(8,128)(2,1)S(1)}, u32[]{:S(2)}) copy-start(bf16[1024,1000]{1,0:T(8,128)(2,1)S(1)} %copy.13.env) | copy-start | bytes 6144004
  67.7 0.9 copy-start.5
  68.6 0.8 copy-start.6
  68.6 0.9 copy-start.7
  69.5 35.6 %all-to-all-start.1 = ((f32[32,8,256]{2,1,0:T(8,128)}), f32[32,8,256]{2,1,0:T(8,128)S(1)}, u32[]{:S(2)}, u32[]{:S(2)}) async-start(f32[32,8,256]{2,1,0:T(8,128)} %bitcast.13), calls=%async_computation.1 | async-start | bytes 524288 | tf_op jit(solution)/shard_map/gram/all_to_all | solution.py:432
  105.2 4.2 %collective-permute-start = (f32[128,1280]{1,0:T(8,128)}, f32[128,1280]{1,0:T(8,128)S(1)}, u32[]{:S(2)}, u32[]{:S(2)}) collective-permute-start(f32[128,1280]{1,0:T(8,128)} %get-tuple-element.19), channel_id=1, source_target_pairs={{0,16},{16,0},{32,48},{48,32},{64,80},{80,64},{96,112},{112,96},{1... | collective-permute-start | bytes 1966088 | tf_op jit(solution)/shard_map/product/ppermute | solution.py:441
  109.4 1.1 copy-start.2
  150.3 64.1 %copy-start.1 = (f32[512,1280]{1,0:T(8,128)S(1)}, f32[512,1280]{1,0:T(8,128)}, u32[]{:S(2)}) copy-start(f32[512,1280]{1,0:T(8,128)} %get-tuple-element.15.design) | copy-start | bytes 7864324
  150.3 64.1 %copy-start.4 = (s32[2]{0:T(128)S(1)}, s32[2]{0:T(128)}, u32[]{:S(2)}) copy-start(s32[2]{0:T(128)} %pad_add_fusion.place) | copy-start | bytes 28
Sparse Core Ops, SparseCore 0:
  10.1 82.2 all-gather.3
